TPU v7x, 32 devices: a whole 2x2x4 slice. The times are simulated.
32 devices in a mesh: section: 2 (over core), shard: 4 (over z), replica: 4 (over y, x).
Axes of the slice: x: 2, y: 2, z: 4, core: 2. Of those that a mesh axis runs over, the one named last changes fastest.
Arguments:
- boundary_in: bfloat16 [2, 2, 16, 577, 1024], P('section', None, ('shard', 'replica')), may hold values from -6 to 6
- counts: int32 [4, 2], replicated, may hold values from 2 to 4, as said below
- w_qkv: bfloat16 [2, 1024, 3, 1024], P('section', None, None, 'shard'), may hold values from -0.1875 to 0.1875
- b_qkv: bfloat16 [2, 2, 1024], P('section', None, 'shard'), may hold values from -1.5 to 1.5
- w_out: bfloat16 [2, 1024, 1024], P('section', 'shard'), may hold values from -0.75 to 0.75
- b_out: bfloat16 [2, 1024], P('section'), may hold values from -1.5 to 1.5
- w_up: bfloat16 [2, 1024, 4096], P('section', None, 'shard'), may hold values from -0.1875 to 0.1875
- b_up: bfloat16 [2, 4096], P('section', 'shard'), may hold values from -2.5 to 2.5
- w_down: bfloat16 [2, 4096, 1024], P('section', 'shard'), may hold values from -0.09375 to 0.09375
- b_down: bfloat16 [2, 1024], P('section'), may hold values from -1.5 to 1.5
- norm1_gain: bfloat16 [2, 1024], P('section'), may hold values from 0.5 to 1.5
- norm1_shift: bfloat16 [2, 1024], P('section'), may hold values from -1 to 1
- norm2_gain: bfloat16 [2, 1024], P('section'), may hold values from 0.5 to 1.5
- norm2_shift: bfloat16 [2, 1024], P('section'), may hold values from -1 to 1
Outputs:
- boundary_out: bfloat16 [2, 2, 16, 577, 1024], P('section', None, ('shard', 'replica'))
- grad_qkv: float32 [2, 1024, 3, 1024], P('section', 'replica', None, 'shard')
- grad_qkv_bias: float32 [2, 2, 1024], P('section', None, ('shard', 'replica'))
- grad_out: float32 [2, 1024, 1024], P('section', 'shard', 'replica')
- grad_out_bias: float32 [2, 1024], P('section', ('shard', 'replica'))
- grad_up: float32 [2, 1024, 4096], P('section', 'replica', 'shard')
- grad_up_bias: float32 [2, 4096], P('section', ('shard', 'replica'))
- grad_down: float32 [2, 4096, 1024], P('section', 'shard', 'replica')
- grad_down_bias: float32 [2, 1024], P('section', ('shard', 'replica'))
- grad_norm1_gain: float32 [2, 1024], P('section', ('shard', 'replica'))
- grad_norm1_shift: float32 [2, 1024], P('section', ('shard', 'replica'))
- grad_norm2_gain: float32 [2, 1024], P('section', ('shard', 'replica'))
- grad_norm2_shift: float32 [2, 1024], P('section', ('shard', 'replica'))
Inputs may be any that keep to these rules, and one draw needn't show every extreme that they name: counts[r, m] is the number of live image slots, the first ones, of replica r in micro-batch m; the values 4 and 2 each occur.
All inputs are finite; a program needn't handle non-finite values.
Results may differ from a plain program's by a relative error of at most 0.02.
Values may be sent and summed in bfloat16 or wider, within the bound.
No kernel may reach another device: no remote copies, remote signals or barrier semaphores. Data moves between devices by JAX's collectives and lax.ppermute only.
A program may use at most 448 MiB of HBM per device.

v0:
```python
import functools

import jax
import jax.numpy as jnp
from jax import lax
from jax.experimental import pallas as pl
from jax.experimental.pallas import tpu as pltpu
from jax.sharding import PartitionSpec as P

HEAD = 64
SEQ = 577
PAD = 592
CHUNK = 144
LOW = jnp.bfloat16
F32 = jnp.float32
ALL_AXES = ("section", "shard", "replica")
NT = (((1,), (1,)), ((), ()))
NN = (((1,), (0,)), ((), ()))
TN = (((0,), (0,)), ((), ()))


def reverse_bits(value, bits):
    flipped = 0
    for spot in range(bits):
        flipped |= ((value >> spot) & 1) << (bits - 1 - spot)
    return flipped


def product(left, right, dims):
    return lax.dot_general(left, right, dims, preferred_element_type=F32)


def row_loop(body):
    whole = PAD // CHUNK

    def step(index, carry):
        body(pl.multiple_of(index * CHUNK, 16), CHUNK)
        return carry

    lax.fori_loop(0, whole, step, 0)
    if PAD % CHUNK:
        body(whole * CHUNK, PAD % CHUNK)


def params(megabytes=48):
    return pltpu.CompilerParams(vmem_limit_bytes=megabytes * 2**20)


def launch(
    lay, kernel, name, scalars, operands, in_specs, out_specs, out_shape, grid, scratch, megabytes, cost=1000
):
    tokens = lay.after
    count = len(scalars) + len(operands)

    def ordered(*refs):
        rest = refs[count + len(tokens) :]
        rest[len(out_shape)][...] = jnp.zeros((8, 128), F32)
        kernel(*refs[:count], *rest[: len(out_shape)], *rest[len(out_shape) + 1 :])

    token_spec = pl.BlockSpec((8, 128), lambda *_: (0, 0))
    results = pl.pallas_call(
        ordered,
        grid_spec=pltpu.PrefetchScalarGridSpec(
            num_scalar_prefetch=len(scalars),
            grid=grid,
            in_specs=list(in_specs) + [pl.BlockSpec(memory_space=pl.ANY)] * len(tokens),
            out_specs=list(out_specs) + [token_spec],
            scratch_shapes=scratch,
        ),
        out_shape=list(out_shape) + [jax.ShapeDtypeStruct((8, 128), F32)],
        compiler_params=params(megabytes),
        cost_estimate=pl.CostEstimate(flops=cost, bytes_accessed=2**18, transcendentals=0),
        name=name,
    )(*scalars, *operands, *tokens)
    lay.after = [results[-1]]
    return results[:-1]


def normalized(values):
    center = values - jnp.mean(values, axis=-1, keepdims=True)
    spread = jnp.mean(center * center, axis=-1, keepdims=True)
    inverse = lax.rsqrt(spread + 1e-06)
    return center * inverse, inverse


class Layout:
    def __init__(self, mesh_shape, width):
        self.shards = mesh_shape["shard"]
        self.replicas = mesh_shape["replica"]
        self.bits = self.replicas.bit_length() - 1
        self.width = width
        self.block = width // self.replicas
        self.flip = [reverse_bits(b, self.bits) for b in range(self.replicas)]
        self.near = self.replicas // 2
        self.slots = 2 * self.shards
        self.after = []

    def absorb(self, *values):
        for value in values:
            corner = value.reshape((-1,) + value.shape[-2:])[0, :8, :128]
            self.after.append(corner)

    def hold(self, *values):
        values, self.after = lax.optimization_barrier((values, self.after))
        return values

    def across_cores(self, value):
        return lax.ppermute(value, "section", [(0, 1), (1, 0)])

    def along_shard(self, value, slot):
        return lax.ppermute(value, "shard", [(i, i ^ slot) for i in range(self.shards)])

    def along_bit_plain(self, value, bit):
        route = [(i, i ^ (1 << bit)) for i in range(self.replicas)]
        return lax.ppermute(value, "replica", route)

    def along_bit(self, value, bit):
        route = []
        for core in range(2):
            physical = bit if core == 0 else self.bits - 1 - bit
            for shard in range(self.shards):
                base = (core * self.shards + shard) * self.replicas
                for replica in range(self.replicas):
                    route.append((base + replica, base + (replica ^ (1 << physical))))
        return lax.ppermute(value, ALL_AXES, route)


def arrange_images(lay, mine, received, blocks, core, live):
    width, block = lay.width, lay.block

    def kernel(scalars, live_ref, mine_ref, other_ref, image_ref, cot_ref):
        here = mine_ref[0]
        there = other_ref[0]
        first = scalars[lay.replicas] == 0
        image = jnp.where(first, here, there)
        cot = jnp.where(first, there, here).astype(F32) * live_ref[0]
        image_ref[...] = jnp.zeros_like(image_ref)
        cot_ref[...] = jnp.zeros_like(cot_ref)
        image_ref[0:SEQ, :] = image
        cot_ref[0:SEQ, :] = cot.astype(LOW)

    scalars = jnp.concatenate([blocks, core[None]]).astype(jnp.int32)
    shape = jax.ShapeDtypeStruct((PAD, width), LOW)
    whole = pl.BlockSpec((1, SEQ, block), lambda b, s: (s[lay.replicas], 0, s[b]))
    return launch(
        lay,
        kernel,
        "arrange_images",
        [scalars],
        [live, mine, received],
        [pl.BlockSpec(memory_space=pltpu.SMEM), whole, whole],
        [pl.BlockSpec((PAD, block), lambda b, s: (0, b))] * 2,
        [shape, shape],
        (lay.replicas,),
        [],
        24,
    )


def restore_image(lay, values, blocks, scale):
    def kernel(scalars, scale_ref, in_ref, out_ref):
        out_ref[...] = (in_ref[0:SEQ, :].astype(F32) * scale_ref[0]).astype(LOW)

    return launch(
        lay,
        kernel,
        "restore_image",
        [blocks],
        [scale, values],
        [
            pl.BlockSpec(memory_space=pltpu.SMEM),
            pl.BlockSpec((PAD, lay.block), lambda b, s: (0, b)),
        ],
        [pl.BlockSpec((SEQ, lay.block), lambda b, s: (0, s[b]))],
        [jax.ShapeDtypeStruct((SEQ, lay.width), LOW)],
        (lay.replicas,),
        [],
        16,
    )[0]


def chosen_half(flag, low, high):
    return jnp.where(flag == 0, low, high)


def arrange_attention(lay, mine, received, scalars):
    rep, block = lay.replicas, lay.block
    part = mine[1].shape[0] // 2

    def kernel(s, qkv_mine, qkv_other, out_mine, out_other, first_ref, second_ref):
        first = s[rep + 2] == 0
        half = s[rep + pl.program_id(0)]

        def columns(ref, t):
            start = 2 * t * part
            return chosen_half(
                half, ref[:, start : start + part], ref[:, start + part : start + 2 * part]
            )

        for t in range(3):
            here, there = columns(qkv_mine, t), columns(qkv_other, t)
            first_ref[0, 0, :, t * part : (t + 1) * part] = jnp.where(first, here, there)
            second_ref[0, 0, :, t * part : (t + 1) * part] = jnp.where(first, there, here)
        here, there = out_mine[...].T, out_other[...].T
        first_ref[0, 0, :, 3 * part :] = jnp.where(first, here, there)
        second_ref[0, 0, :, 3 * part :] = jnp.where(first, there, here)

    shape = jax.ShapeDtypeStruct((2, rep, block, 4 * part), LOW)
    qkv_spec = pl.BlockSpec((block, 6 * part), lambda p, b, s: (s[b], 0))
    out_spec = pl.BlockSpec((part, block), lambda p, b, s: (s[rep + p], s[b]))
    return launch(
        lay,
        kernel,
        "arrange_attention",
        [scalars],
        [mine[0], received[0], mine[1], received[1]],
        [qkv_spec, qkv_spec, out_spec, out_spec],
        [pl.BlockSpec((1, 1, block, 4 * part), lambda p, b, s: (p, b, 0, 0))] * 2,
        [shape, shape],
        (2, rep),
        [],
        16,
    )


def arrange_dense(lay, mine, received, scalars):
    rep, block = lay.replicas, lay.block
    part = mine[0].shape[1] // 2

    def kernel(s, up_mine, up_other, down_mine, down_other, first_ref, second_ref):
        first = s[rep + 2] == 0
        here, there = up_mine[...], up_other[...]
        first_ref[0, 0, :, :part] = jnp.where(first, here, there)
        second_ref[0, 0, :, :part] = jnp.where(first, there, here)
        here, there = down_mine[...].T, down_other[...].T
        first_ref[0, 0, :, part:] = jnp.where(first, here, there)
        second_ref[0, 0, :, part:] = jnp.where(first, there, here)

    shape = jax.ShapeDtypeStruct((2, rep, block, 2 * part), LOW)
    up_spec = pl.BlockSpec((block, part), lambda p, b, s: (s[b], s[rep + p]))
    down_spec = pl.BlockSpec((part, block), lambda p, b, s: (s[rep + p], s[b]))
    return launch(
        lay,
        kernel,
        "arrange_dense",
        [scalars],
        [mine[0], received[0], mine[1], received[1]],
        [up_spec, up_spec, down_spec, down_spec],
        [pl.BlockSpec((1, 1, block, 2 * part), lambda p, b, s: (p, b, 0, 0))] * 2,
        [shape] * 2,
        (2, rep),
        [],
        16,
    )


def first_pieces(lay, qkv, out, up, down, scalars):
    rep, block = lay.replicas, lay.block
    part, wide = out.shape[0] // 2, up.shape[1] // 2

    def kernel(s, qkv_ref, out_ref, up_ref, down_ref, *outs):
        core = s[rep + 2]
        for flag, attention_ref, dense_ref in ((core, *outs[:2]), (1 - core, *outs[2:])):
            for t in range(3):
                start = 2 * t * part
                attention_ref[:, t * part : (t + 1) * part] = chosen_half(
                    flag,
                    qkv_ref[:, start : start + part],
                    qkv_ref[:, start + part : start + 2 * part],
                )
            attention_ref[:, 3 * part :] = chosen_half(flag, out_ref[:part], out_ref[part:]).T
            dense_ref[:, :wide] = chosen_half(flag, up_ref[:, :wide], up_ref[:, wide:])
            dense_ref[:, wide:] = chosen_half(flag, down_ref[:wide], down_ref[wide:]).T

    attention_shape = jax.ShapeDtypeStruct((block, 4 * part), LOW)
    dense_shape = jax.ShapeDtypeStruct((block, 2 * wide), LOW)
    attention_spec = pl.BlockSpec((block, 4 * part), lambda i, s: (0, 0))
    dense_spec = pl.BlockSpec((block, 2 * wide), lambda i, s: (0, 0))
    return launch(
        lay,
        kernel,
        "first_pieces",
        [scalars],
        [qkv, out, up, down],
        [
            pl.BlockSpec((block, 6 * part), lambda i, s: (s[0], 0)),
            pl.BlockSpec((2 * part, block), lambda i, s: (0, s[0])),
            pl.BlockSpec((block, 2 * wide), lambda i, s: (s[0], 0)),
            pl.BlockSpec((2 * wide, block), lambda i, s: (0, s[0])),
        ],
        [attention_spec, dense_spec] * 2,
        [attention_shape, dense_shape] * 2,
        (1,),
        [],
        16,
    )


def pick_slots(lay, gathered, slot_order):
    rows, columns = gathered.shape[1:]

    def kernel(_, in_ref, out_ref):
        out_ref[0] = in_ref[...]

    return launch(
        lay,
        kernel,
        "pick_slots",
        [slot_order],
        [gathered],
        [pl.BlockSpec((1, rows, columns), lambda k, s: (s[k + 1], 0, 0))],
        [pl.BlockSpec((1, 1, rows, columns), lambda k, s: (0, k, 0, 0))],
        [jax.ShapeDtypeStruct((1, lay.shards - 1, rows, columns), LOW)],
        (lay.shards - 1,),
        [],
        8,
    )[0]


def join(lay, first, second):
    count, rows = first.shape[0], first.shape[1]
    shape = (2 * count,) + first.shape[1:]
    block = (1, rows) + first.shape[2:]

    def kernel(first_ref, second_ref, out_ref):
        step = pl.program_id(0)

        @pl.when(step < count)
        def _():
            out_ref[...] = first_ref[...]

        @pl.when(step >= count)
        def _():
            out_ref[...] = second_ref[...]

    return launch(
        lay,
        kernel,
        "join",
        [],
        [first, second],
        [
            pl.BlockSpec(block, lambda i: (jnp.minimum(i, count - 1), 0, 0, 0)),
            pl.BlockSpec(block, lambda i: (jnp.maximum(i - count, 0), 0, 0, 0)),
        ],
        [pl.BlockSpec(block, lambda i: (i, 0, 0, 0))],
        [jax.ShapeDtypeStruct(shape, LOW)],
        (2 * count,),
        [],
        16,
    )[0]


def copied(lay, value):
    def kernel(in_ref, out_ref):
        out_ref[...] = in_ref[...]

    spec = pl.BlockSpec(value.shape, lambda i: (0, 0))
    shape = jax.ShapeDtypeStruct(value.shape, value.dtype)
    return launch(lay, kernel, "copied", [], [value], [spec], [spec], [shape], (1,), [], 8)[0]


class Gather:
    def __init__(self, lay, slot_order, pieces):
        self.lay, self.pieces, self.slot_order = lay, pieces, slot_order
        self.state = [None] * len(pieces)
        self.done = [0] * len(pieces)

    def start(self, n):
        piece = self.pieces[n] if n == 0 else copied(self.lay, self.pieces[n])
        self.state[n] = lax.all_gather(piece, "shard")

    def step(self, n):
        lay = self.lay
        if self.done[n] == 0:
            near = pick_slots(lay, self.state[n], self.slot_order)
        else:
            near = join(lay, *self.state[n])
        self.state[n] = (near, lay.along_bit(near, self.done[n]))
        self.done[n] += 1

    def finish(self, n, own):
        lay = self.lay
        while self.done[n] < lay.bits:
            self.step(n)
        near, far = self.state[n]
        (far,) = lay.hold(far)
        return (own, near, far, lay.across_cores(near), lay.across_cores(far))


def fetch_weights(lay, refs, held, sems, slot):
    own, near, far, near_other, far_other = refs
    half = lay.near
    side, k = divmod(slot, lay.shards)

    def start(source, target):
        pltpu.make_async_copy(source, target, sems.at[slot]).start()

    if k == 0:
        start(own.at[side], held.at[slot])
    elif side == 0:
        start(near.at[:, k - 1], held.at[slot, 0:half])
        start(far.at[:, k - 1], held.at[slot, half : 2 * half])
    else:
        for b in range(half):
            start(near_other.at[b, k - 1], held.at[slot, lay.flip[b]])
            start(far_other.at[b, k - 1], held.at[slot, lay.flip[half + b]])


def await_weights(held, sems, slot):
    pltpu.make_async_copy(held.at[slot], held.at[slot], sems.at[slot]).wait()


def flat(block):
    return block.reshape(block.shape[0] * block.shape[1], block.shape[2])


def layer_call(lay, kernel, name, weights, slotted, whole, late, rows, outs, megabytes):
    slots, width, shards = lay.slots, lay.width, lay.shards
    once = dict(pipeline_mode=pl.Buffered(1))

    def own_half(i):
        return (jnp.minimum(i, shards), 0, 0)

    def other_half(i):
        return (jnp.where(i < shards, shards, i - shards), 0, 0)

    def spec(shape, **mode):
        if len(shape) == 3:
            return pl.BlockSpec((1,) + shape[1:], lambda i: (i, 0, 0))
        return pl.BlockSpec(shape, lambda i: (0, 0), **mode)

    out_specs, out_shape = [], []
    for o in outs:
        if len(o.shape) == 3 and o.shape[0] == shards + 1:
            out_specs += [pl.BlockSpec((1,) + o.shape[1:], m) for m in (own_half, other_half)]
            out_shape += [o, o]
        else:
            out_specs.append(spec(o.shape))
            out_shape.append(o)
    outs = out_shape
    anywhere = pl.BlockSpec(memory_space=pltpu.HBM)
    counts = [5 * len(weights), len(slotted), len(whole), len(late), len(rows), len(outs)]

    def body(*refs):
        groups, at = [], 0
        for count in counts + [1, len(weights), len(weights), len(late)]:
            groups.append(refs[at : at + count])
            at += count
        arrays, slot_refs, whole_refs, late_refs, row_refs, out_refs = groups[:6]
        (total,), held, sems, late_held = groups[6:10]
        late_sem = refs[at] if late else None
        step = pl.program_id(0)

        def late_copy(n):
            return pltpu.make_async_copy(late_refs[n], late_held[n], late_sem.at[n])

        @pl.when(step == 0)
        def _():
            for slot in range(slots):
                for n in range(len(weights)):
                    fetch_weights(lay, arrays[5 * n : 5 * n + 5], held[n], sems[n], slot)
            for n in range(len(late)):
                late_copy(n).start()

        def weight(n):
            await_weights(held[n], sems[n], step)
            return flat(held[n][step])

        def late_values():
            for n in range(len(late)):
                late_copy(n).wait()
            return late_held

        kernel(step, weight, slot_refs, whole_refs, late_values, row_refs, out_refs, total)

    arrays = [array for matrix in weights for array in matrix]
    scratch = [pltpu.VMEM((PAD, width), F32)]
    scratch += [pltpu.VMEM((slots,) + matrix[0].shape[1:], LOW) for matrix in weights]
    scratch += [pltpu.SemaphoreType.DMA((slots,)) for _ in weights]
    scratch += [pltpu.VMEM(a.shape, a.dtype) for a in late]
    if late:
        scratch.append(pltpu.SemaphoreType.DMA((len(late),)))
    return launch(
        lay,
        body,
        name,
        [],
        [*arrays, *slotted, *whole, *late, *rows],
        [anywhere] * len(arrays)
        + [spec(a.shape) for a in slotted]
        + [spec(a.shape, **once) for a in whole]
        + [anywhere] * len(late)
        + [spec(a.shape, **once) for a in rows],
        out_specs,
        out_shape,
        (slots,),
        scratch,
        megabytes,
    )


def add_product(lay, step, total, acts, matrix):
    for b in range(lay.replicas):
        columns = slice(b * lay.block, (b + 1) * lay.block)
        term = product(acts, matrix[columns], NT)
        total[:, columns] = jnp.where(step == 0, 0.0, total[:, columns]) + term


def low_shape(*shape):
    return jax.ShapeDtypeStruct(shape, LOW)


def wide_shape(*shape):
    return jax.ShapeDtypeStruct(shape, F32)


def mask_keys(scores, low):
    edge = SEQ // 16 * 16
    valid = lax.broadcasted_iota(jnp.int32, (PAD - edge, 1), 0) < SEQ - edge
    return jnp.concatenate([scores[:edge], jnp.where(valid, scores[edge:], low)], axis=0)


def attend(block, part):
    query, keys, values = block[:, :part], block[:, part : 2 * part], block[:, 2 * part :]
    heads = range(part // HEAD)
    lanes = lax.broadcasted_iota(jnp.int32, (1, part), 1) // HEAD
    query = query * HEAD ** (-0.5)
    turned = values.T
    ones = jnp.ones((16, PAD), LOW)
    scores = [product(keys, jnp.where(lanes == h, query, 0), NT) for h in heads]
    scores = [mask_keys(score, -1e30) for score in scores]
    peaks = [jnp.max(score, axis=0, keepdims=True) for score in scores]
    weights = [jnp.exp(score - peak).astype(LOW) for score, peak in zip(scores, peaks)]
    sums = [
        product(jnp.concatenate([turned[h * HEAD : (h + 1) * HEAD], ones], axis=0), weights[h], NN)
        for h in heads
    ]
    result = jnp.concatenate([s[:HEAD] / s[HEAD : HEAD + 1] for s in sums], axis=0).T
    spot = lax.broadcasted_iota(jnp.int32, (8, 1), 0)
    logs = jnp.zeros((8, PAD), F32)
    for h in heads:
        logs = jnp.where(spot == h, peaks[h] + jnp.log(sums[h][HEAD : HEAD + 1]), logs)
    return result.astype(LOW), logs


def attend_back(block, grads, attended, logs, part):
    query, keys, values = block[:, :part], block[:, part : 2 * part], block[:, 2 * part :]
    heads = range(part // HEAD)
    lanes = lax.broadcasted_iota(jnp.int32, (1, part), 1) // HEAD
    wide = lax.broadcasted_iota(jnp.int32, (1, 128), 1)
    query = query * HEAD ** (-0.5)

    def pick(h, array):
        return jnp.where(lanes == h, array, 0)

    along = grads.astype(F32) * attended.astype(F32)
    inner = jnp.zeros((PAD, 128), F32)
    for h in heads:
        inner = jnp.where(wide == h, jnp.sum(pick(h, along), axis=-1, keepdims=True), inner)
    inner = inner.T
    scores = [product(keys, pick(h, query), NT) for h in heads]
    slopes = [product(values, pick(h, grads), NT) for h in heads]
    chances = [mask_keys(jnp.exp(scores[h] - logs[h : h + 1]), 0.0) for h in heads]
    grad_scores = [(chances[h] * (slopes[h] - inner[h : h + 1])).astype(LOW) for h in heads]
    low = [chance.astype(LOW) for chance in chances]
    value_terms = [product(low[h], grads, NN) for h in heads]
    key_terms = [product(grad_scores[h], query, NN) for h in heads]
    turned = keys.T
    query_terms = [
        product(turned[h * HEAD : (h + 1) * HEAD], grad_scores[h], NN) for h in heads
    ]

    def merge(terms):
        result = terms[0]
        for h in heads:
            result = jnp.where(lanes == h, terms[h], result)
        return result

    return (
        jnp.concatenate(query_terms, axis=0).T * HEAD ** (-0.5),
        merge(key_terms),
        merge(value_terms),
    )


def norm_back(values, grads, gain):
    values, inverse = normalized(values)
    slope = grads * gain
    mean = jnp.mean(slope, axis=-1, keepdims=True)
    along = jnp.mean(slope * values, axis=-1, keepdims=True)
    term = inverse * (slope - mean - values * along)
    return (
        term,
        jnp.sum(grads * values, axis=0, keepdims=True),
        jnp.sum(grads, axis=0, keepdims=True),
    )


def attention_forward(lay, entry, weights, bias, rows):
    slots, width = lay.slots, lay.width
    part = weights[0].shape[3] // 4

    def kernel(step, weight, slotted, whole, late, rows, outs, total):
        normed, mixed, attended, logs, middle, normed_two = outs

        @pl.when(step == 0)
        def _():
            def norm_rows(start, count):
                values, _ = normalized(whole[0][pl.ds(start, count), :].astype(F32))
                normed[pl.ds(start, count), :] = (values * rows[0][...] + rows[1][...]).astype(LOW)

            row_loop(norm_rows)

        matrix = weight(0)
        block = (product(normed[...], matrix[:, : 3 * part], NN) + slotted[0][0]).astype(LOW)
        mixed[0] = block
        result, log_rows = attend(block, part)
        attended[0] = result
        logs[0] = log_rows
        add_product(lay, step, total, result, matrix[:, 3 * part :])

        @pl.when(step == slots - 1)
        def _():
            def finish(start, count):
                at = pl.ds(start, count)
                sums = whole[0][at, :].astype(F32) + total[at, :] + rows[2][...]
                middle[at, :] = sums
                values, _ = normalized(sums)
                normed_two[at, :] = (values * rows[3][...] + rows[4][...]).astype(LOW)

            row_loop(finish)

    return layer_call(
        lay,
        kernel,
        "attention_forward",
        [weights],
        [bias],
        [entry],
        [],
        rows,
        [
            low_shape(PAD, width),
            low_shape(slots, PAD, 3 * part),
            low_shape(slots, PAD, part),
            wide_shape(slots, 8, PAD),
            wide_shape(PAD, width),
            low_shape(PAD, width),
        ],
        40,
    )


def dense_forward(lay, normed_two, middle, weights, bias, b_down):
    slots, width = lay.slots, lay.width
    size = weights[0].shape[3] // 2

    def kernel(step, weight, slotted, whole, late, rows, outs, total):
        active, active_sent, slope, result = outs
        matrix = weight(0)
        hidden = product(whole[0][...], matrix[:, :size], NN) + slotted[0][0]
        chance = 0.5 + 0.5 * lax.erf(hidden * (0.5**0.5))
        density = jnp.exp(-0.5 * hidden * hidden) * 0.3989422804014327
        low = (hidden * chance).astype(LOW)
        active[0] = low
        active_sent[0] = low
        slope[0] = (chance + hidden * density).astype(LOW)
        add_product(lay, step, total, low, matrix[:, size:])

        @pl.when(step == slots - 1)
        def _():
            (middle_ref,) = late()
            result[...] = (middle_ref[...] + total[...] + rows[0][...]).astype(LOW)

    return layer_call(
        lay,
        kernel,
        "dense_forward",
        [weights],
        [bias],
        [normed_two],
        [middle],
        [b_down],
        [
            low_shape(lay.shards + 1, PAD, size),
            low_shape(slots, PAD, size),
            low_shape(PAD, width),
        ],
        46,
    )


def dense_backward(lay, tangent, slope, middle, weights, gain_two):
    slots, width = lay.slots, lay.width
    size = weights[0].shape[3] // 2

    def kernel(step, weight, slotted, whole, late, rows, outs, total):
        grad_hidden, hidden_sent, up_sums, grad_middle, grad_branch = outs[:5]
        down_sums, gains, shifts, out_sums = outs[5:]

        @pl.when(step == 0)
        def _():
            down_sums[...] = jnp.sum(whole[0][...].astype(F32), axis=0, keepdims=True)
            for ref in (gains, shifts, out_sums):
                ref[...] = jnp.zeros_like(ref)

        matrix = weight(0)
        grad = product(whole[0][...], matrix[:, size:], NN).astype(LOW).astype(F32)
        grad = (grad * slotted[0][0].astype(F32)).astype(LOW)
        grad_hidden[0] = grad
        hidden_sent[0] = grad
        up_sums[0] = jnp.sum(grad.astype(F32), axis=0, keepdims=True)
        add_product(lay, step, total, grad, matrix[:, :size])

        @pl.when(step == slots - 1)
        def _():
            (middle,) = late()

            def finish(start, count):
                at = pl.ds(start, count)
                term, gain_part, shift_part = norm_back(middle[at, :], total[at, :], rows[0][...])
                sums = whole[0][at, :].astype(F32) + term
                grad_middle[at, :] = sums
                grad_branch[at, :] = sums.astype(LOW)
                gains[...] += gain_part
                shifts[...] += shift_part
                out_sums[...] += jnp.sum(sums, axis=0, keepdims=True)

            row_loop(finish)

    row = wide_shape(1, width)
    return layer_call(
        lay,
        kernel,
        "dense_backward",
        [weights],
        [slope],
        [tangent],
        [middle],
        [gain_two],
        [
            low_shape(lay.shards + 1, PAD, size),
            wide_shape(slots, 1, size),
            wide_shape(PAD, width),
            low_shape(PAD, width),
            row,
            row,
            row,
            row,
        ],
        48,
    )


def attention_backward(
    lay, grad_branch, mixed, attended, logs, entry, grad_middle, weights, gain_one
):
    slots, width = lay.slots, lay.width
    part = weights[0].shape[3] // 4

    def kernel(step, weight, slotted, whole, late, rows, outs, total):
        grad_mixed, mixed_sent, qkv_sums, grad_entry, gains, shifts = outs

        @pl.when(step == 0)
        def _():
            for ref in (gains, shifts):
                ref[...] = jnp.zeros_like(ref)

        matrix = weight(0)
        upstream = product(whole[0][...], matrix[:, 3 * part :], NN).astype(LOW)
        parts = attend_back(slotted[0][0], upstream, slotted[1][0], slotted[2][0], part)
        for spot, term in enumerate(parts):
            columns = slice(spot * part, (spot + 1) * part)
            rounded = term.astype(LOW)
            grad_mixed[0, :, columns] = rounded
            mixed_sent[0, :, columns] = rounded
            qkv_sums[0, :, columns] = jnp.sum(rounded.astype(F32), axis=0, keepdims=True)
        add_product(lay, step, total, grad_mixed[0], matrix[:, : 3 * part])

        @pl.when(step == slots - 1)
        def _():
            entry, grad_middle = late()

            def finish(start, count):
                at = pl.ds(start, count)
                term, gain_part, shift_part = norm_back(
                    entry[at, :].astype(F32), total[at, :], rows[0][...]
                )
                grad_entry[at, :] = (grad_middle[at, :] + term).astype(LOW)
                gains[...] += gain_part
                shifts[...] += shift_part

            row_loop(finish)

    row = wide_shape(1, width)
    return layer_call(
        lay,
        kernel,
        "attention_backward",
        [weights],
        [mixed, attended, logs],
        [grad_branch],
        [entry, grad_middle],
        [gain_one],
        [
            low_shape(lay.shards + 1, PAD, 3 * part),
            wide_shape(slots, 1, 3 * part),
            low_shape(PAD, width),
            row,
            row,
        ],
        48,
    )


def weight_grads(lay, slot_order, pairs, cost):
    half, block, shards, width = lay.near, lay.block, lay.shards, lay.width
    sizes = [pair[2].shape[2] for pair in pairs]
    total = sum(sizes)
    whole = pl.BlockSpec((PAD, width), lambda k, s: (0, 0), pipeline_mode=pl.Buffered(1))
    specs, operands, scratch = [], [], []
    for x, x_other, feats, feats_other in pairs:
        feature_spec = pl.BlockSpec((1, PAD, feats.shape[2]), lambda k, s: (k, 0, 0))
        specs += [whole, whole, feature_spec, feature_spec]
        operands += [x, x_other, feats, feats_other]
        scratch += [pltpu.VMEM((width, PAD), LOW)] * 2

    def kernel(_, *refs):
        far_ref, near_ref = refs[4 * len(pairs) : 4 * len(pairs) + 2]
        turned = refs[4 * len(pairs) + 2 :]

        @pl.when(pl.program_id(0) == 0)
        def _():
            for n in range(len(pairs)):
                for b in range(lay.replicas):
                    rows = slice(b * block, (b + 1) * block)
                    other = slice(lay.flip[b] * block, (lay.flip[b] + 1) * block)
                    turned[2 * n][rows, :] = refs[4 * n][:, rows].T
                    turned[2 * n + 1][rows, :] = refs[4 * n + 1][:, other].T

        start = 0
        for n, size in enumerate(sizes):
            grads = product(turned[2 * n][...], refs[4 * n + 2][0], NN) + product(
                turned[2 * n + 1][...], refs[4 * n + 3][0], NN
            )
            grads = grads.reshape(2 * half, block, size).astype(LOW)
            near_ref[:, 0, :, start : start + size] = grads[:half]
            far_ref[:, 0, :, start : start + size] = grads[half:]
            start += size

    return launch(
        lay,
        kernel,
        "weight_grads",
        [slot_order],
        operands,
        specs,
        [pl.BlockSpec((half, 1, block, total), lambda k, s: (0, s[k], 0, 0))] * 2,
        [low_shape(half, shards, block, total)] * 2,
        (shards,),
        scratch,
        28,
        cost,
    )


def add_blocks(lay, *groups, cost=10**10):
    count = min(array.shape[0] - start for group in groups for array, start in group)
    widths = [group[0][0].shape[3] for group in groups]
    middle = groups[0][0][0].shape[1:3]

    def kernel(*refs):
        at, column = 0, 0
        for group, width in zip(groups, widths):
            total = refs[at][...].astype(F32)
            for ref in refs[at + 1 : at + len(group)]:
                total = total + ref[...].astype(F32)
            refs[-1][..., column : column + width] = total.astype(LOW)
            at, column = at + len(group), column + width

    def spec(start, width):
        return pl.BlockSpec((1,) + middle + (width,), lambda i: (i + start, 0, 0, 0))

    return launch(
        lay,
        kernel,
        "add_blocks",
        [],
        [array for group in groups for array, _ in group],
        [spec(start, width) for group, width in zip(groups, widths) for _, start in group],
        [spec(0, sum(widths))],
        [jax.ShapeDtypeStruct((count,) + middle + (sum(widths),), LOW)],
        (count,),
        [],
        28,
        cost,
    )[0]


def pause(lay, cost=4 * 10**10):
    def kernel(out_ref):
        out_ref[...] = jnp.zeros_like(out_ref)

    spec = pl.BlockSpec((8, 128), lambda i: (0, 0))
    shape = jax.ShapeDtypeStruct((8, 128), F32)
    launch(lay, kernel, "pause", [], [], [], [spec], [shape], (1,), [], 8, cost)


def pack_vectors(lay, sums, blocks, slot_order, core):
    rep, block, shards = lay.replicas, lay.block, lay.shards
    assert rep == shards
    wide = sums[0][1].shape[2]
    operands = [v for layer in (0, 1) for v in (*sums[layer][0], *sums[layer][1:])]

    def kernel(s, *refs):
        keep_ref, send_ref = refs[16:]
        owner = s[rep + shards]
        keep_ref[...] = jnp.zeros_like(keep_ref)
        send_ref[...] = jnp.zeros_like(send_ref)
        here, there = refs[:8], refs[8:16]

        def chosen(n, index, mine):
            first = (owner == 0) if mine else (owner != 0)
            return jnp.where(first, here[n][index], there[n][index])

        for out_ref, mine in ((keep_ref, True), (send_ref, False)):
            for n in range(6):
                for b in range(rep):
                    columns = slice(b * block, (b + 1) * block)
                    value = chosen(n, (slice(None), columns), mine)
                    out_ref[s[b] ^ s[rep], n : n + 1, :block] = value
            for side in range(2):
                half = side ^ owner
                for k in range(shards):
                    slot = side * shards + k
                    ups = chosen(6, slot, mine)
                    parts = chosen(7, slot, mine)
                    out_ref[k, pl.ds(8 + half, 1), :] = ups
                    out_ref[k, pl.ds(6 + half, 1), : parts.shape[1]] = parts

    def spec(array):
        return pl.BlockSpec(array.shape, lambda i, s, n=array.ndim: (0,) * n)

    scalars = jnp.concatenate([blocks, slot_order, core[None]])
    shape = jax.ShapeDtypeStruct((shards, 16, wide), F32)
    keep, send = launch(
        lay,
        kernel,
        "pack_vectors",
        [scalars],
        operands,
        [spec(v) for v in operands],
        [pl.BlockSpec(shape.shape, lambda i, s: (0, 0, 0))] * 2,
        [shape] * 2,
        (1,),
        [],
        8,
    )
    return keep, send


def shards(
    boundary_in,
    counts,
    w_qkv,
    b_qkv,
    w_out,
    b_out,
    w_up,
    b_up,
    w_down,
    b_down,
    norm1_gain,
    norm1_shift,
    norm2_gain,
    norm2_shift,
):
    width = boundary_in.shape[4]
    sizes = {axis: lax.axis_size(axis) for axis in ALL_AXES}
    lay = Layout(sizes, width)
    core = lax.axis_index("section").astype(jnp.int32)
    shard = lax.axis_index("shard").astype(jnp.int32)
    replica = lax.axis_index("replica").astype(jnp.int32)
    on_first = core == 0
    heads_wide = w_qkv.shape[3]
    part = heads_wide // 2
    ff_part = w_up.shape[2] // 2
    positions = jnp.arange(lay.replicas, dtype=jnp.int32)
    flips = jnp.asarray(lay.flip, jnp.int32)
    blocks = jnp.where(on_first, positions, flips) ^ replica
    inverse_blocks = jnp.where(on_first, positions ^ replica, flips[positions ^ replica])
    halves = jnp.arange(2, dtype=jnp.int32) ^ core
    scalars = jnp.concatenate([blocks, halves, core[None]])

    slot_order = jnp.arange(lay.shards, dtype=jnp.int32) ^ shard

    raw_qkv = w_qkv[0].reshape(width, 6 * part)
    raw_out, raw_up, raw_down = w_out[0], w_up[0], w_down[0]
    split_pieces = first_pieces(lay, raw_qkv, raw_out, raw_up, raw_down, scalars)
    first, second = [], []
    for piece, sent in zip(split_pieces[:2], split_pieces[2:]):
        other = lay.across_cores(sent)
        first.append(jnp.where(on_first, piece, other))
        second.append(jnp.where(on_first, other, piece))
    pieces = first + second
    (pictures,) = lay.hold(boundary_in[0, :, 0])
    received = lay.across_cores(pictures)
    live = (shard < counts[replica, core]).astype(F32)[None]
    gather = Gather(lay, slot_order, pieces)
    gather.start(0)
    image, cot = arrange_images(lay, pictures, received, blocks, core, live)

    raws = (raw_qkv, raw_out, raw_up, raw_down)
    raws_other = [lay.across_cores(raw) for raw in raws]
    own_attention = arrange_attention(lay, raws[:2], raws_other[:2], scalars)

    packed = jnp.concatenate(
        [v[0] for v in (b_out, b_down, norm1_gain, norm1_shift, norm2_gain, norm2_shift)]
        + [b_qkv.reshape(-1), b_up.reshape(-1)]
    )
    packed_other = lay.across_cores(packed)
    both = jnp.stack(
        [jnp.where(on_first, packed, packed_other), jnp.where(on_first, packed_other, packed)]
    )
    wide = both[:, : 6 * width].reshape(2, 6, lay.replicas, lay.block)
    wide = jnp.take(wide, blocks, axis=2).reshape(2, 6, 1, width).astype(F32)
    split = both[:, 6 * width :]
    split = jnp.stack([split] + [lay.along_shard(split, k) for k in range(1, lay.shards)])
    split_qkv = split[:, :, : 4 * part].reshape(lay.shards, 2, 2, 2, part)
    split_qkv = jnp.take(split_qkv, halves, axis=3).transpose(1, 3, 0, 2, 4)
    split_qkv = split_qkv.reshape(2, lay.slots, 2, part)
    bias_qkv = jnp.concatenate(
        [split_qkv[:, :, 0], jnp.zeros_like(split_qkv[:, :, 0]), split_qkv[:, :, 1]], axis=-1
    ).reshape(2, lay.slots, 1, 3 * part).astype(F32)
    bias_up = split[:, :, 4 * part :].reshape(lay.shards, 2, 2, ff_part)
    bias_up = jnp.take(bias_up, halves, axis=2).transpose(1, 2, 0, 3)
    bias_up = bias_up.reshape(2, lay.slots, 1, ff_part).astype(F32)

    kept, weights = [], []
    entry = image
    gather.step(0)
    gather.start(1)
    gather.step(0)
    gather.start(2)
    gather.step(1)
    gather.start(3)
    w_attention = gather.finish(0, own_attention[0])
    for layer in range(2):
        vec_out, vec_down, gain_one, shift_one, gain_two, shift_two = wide[layer]
        normed, mixed, attended, logs, middle, normed_two = attention_forward(
            lay,
            entry,
            w_attention,
            bias_qkv[layer],
            (gain_one, shift_one, vec_out, gain_two, shift_two),
        )
        exchanged = [
            lay.across_cores(value) for value in (normed, normed_two, attended[lay.shards :])
        ]
        if layer == 0:
            gather.step(1)
            gather.step(2)
            lay.absorb(*exchanged)
            own_dense = arrange_dense(lay, raws[2:], raws_other[2:], scalars)
            gather.step(3)
            w_dense = gather.finish(1, own_dense[0])
            gather.step(2)
            pause(lay)
        else:
            w_dense = gather.finish(3, own_dense[1])
            lay.absorb(kept[0][-1][-1])
            pause(lay)
        active, active_sent, slope, result = dense_forward(
            lay,
            normed_two,
            middle,
            w_dense,
            bias_up[layer],
            vec_down,
        )
        weights.append((w_attention, w_dense))
        exchanged.append(lay.across_cores(active_sent))
        if layer == 0:
            w_attention = gather.finish(2, own_attention[1])
            gather.step(3)
            pause(lay)
        kept.append(
            (entry, normed, mixed, attended, logs, middle, normed_two, active, slope, exchanged)
        )
        entry = result

    terms, sums, vector_sums, latest = {}, {}, {}, {}

    def begin(name, *pairs, cost=1000):
        far, near = weight_grads(lay, slot_order, pairs, cost)
        arrived = lay.along_bit(far, lay.bits - 1)
        terms[name] = [(near, 0), (arrived, 0)]

    def halve(name, cost=10**10):
        for bit in range(lay.bits - 2, -1, -1):
            split = 1 << bit
            group = [(array, start + split) for array, start in terms[name]]
            sent = add_blocks(lay, group, cost=cost)
            terms[name] = terms[name] + [(lay.along_bit(sent, bit), 0)]

    def collect(names, direct, cost=10**10):
        total = add_blocks(lay, *(terms[name] for name in names), cost=cost)[0]
        if direct:
            latest[names] = lax.all_to_all(total, "shard", 0, 0, tiled=True)
        else:
            latest[names] = lax.psum_scatter(total, "shard", scatter_dimension=0)[None]

    def settle(*all_names):
        for names, total in zip(all_names, lay.hold(*(latest[names] for names in all_names))):
            spread(names, total)

    def spread(names, total):
        total = jnp.sum(total.astype(F32), axis=0)
        at = 0
        for name in names:
            size = terms[name][0][0].shape[3]
            sums[name] = total[:, at : at + size]
            at += size

    tangent = cot
    for layer in (1, 0):
        w_attention, w_dense = weights[layer]
        vec_out, vec_down, gain_one, shift_one, gain_two, shift_two = wide[layer]
        entry_in, normed, mixed, attended, logs, middle, normed_two, active, slope, other = kept[layer]
        normed_other, normed_two_other, attended_other, active_other = other
        if layer == 1:
            begin((1, "down"), (tangent, lay.across_cores(tangent), active, active_other))
        (
            grad_hidden,
            hidden_sent,
            up_sums,
            grad_middle,
            grad_branch,
            down_sums,
            gain_two_sum,
            shift_two_sum,
            out_sums,
        ) = dense_backward(lay, tangent, slope, middle, w_dense, gain_two)
        branch_other, hidden_other = lay.across_cores(grad_branch), lay.across_cores(hidden_sent)
        out_pair = (grad_branch, branch_other, attended, attended_other)
        if layer == 1:
            halve((1, "down"))
        else:
            settle(((1, "down"),))
            collect(((1, "out"), (1, "up")), False)
            halve((0, "down"))
        begin((layer, "out"), out_pair, cost=4 * 10**10)
        if layer == 0:
            halve((1, "qkv"))
        begin((layer, "up"), (normed_two, normed_two_other, grad_hidden, hidden_other))
        if layer == 0:
            collect(((1, "qkv"), (0, "down")), True)
        grad_mixed, mixed_sent, qkv_sums, grad_entry, gain_one_sum, shift_one_sum = (
            attention_backward(
                lay,
                grad_branch,
                mixed,
                attended,
                logs,
                entry_in,
                grad_middle,
                w_attention,
                gain_one,
            )
        )
        tangent = grad_entry
        mixed_other = lay.across_cores(mixed_sent)
        vector_sums[layer] = (
            [out_sums, down_sums, gain_one_sum, shift_one_sum, gain_two_sum, shift_two_sum],
            up_sums,
            qkv_sums,
        )
        if layer == 1:
            collect(((1, "down"),), False)
        if layer == 0:
            keep, send = pack_vectors(lay, vector_sums, blocks, slot_order, core)
            send = lay.across_cores(send)
        halve((layer, "out"))
        if layer == 0:
            (send,) = lay.hold(send)
            summed = keep + send
            coming = [lay.along_shard(summed[k], k) for k in range(1, lay.shards)]
        halve((layer, "up"))
        if layer == 0:
            settle(((1, "out"), (1, "up")), ((1, "qkv"), (0, "down")))
            pause(lay, 10**10)
        if layer == 1:
            active, active_other = kept[0][7], kept[0][9][3]
            begin((0, "down"), (tangent, lay.across_cores(tangent), active, active_other))
        begin((layer, "qkv"), (normed, normed_other, grad_mixed, mixed_other))
    summed = sum(lay.hold(*coming), summed[0])
    coming = lay.along_bit_plain(summed, 0)
    back = restore_image(lay, tangent, blocks, jnp.ones((1,), F32))
    ahead = restore_image(lay, entry, blocks, live)
    collect(((0, "out"), (0, "up")), False, cost=2 * 10**10)
    halve((0, "qkv"), cost=1000)
    back, ahead = lay.hold(back, ahead)
    for bit in range(lay.bits):
        (coming,) = lay.hold(coming)
        summed = summed + coming
        if bit + 1 < lay.bits:
            coming = lay.along_bit_plain(summed, bit + 1)
    collect(((0, "qkv"),), True, cost=1000)
    last = (((0, "out"), (0, "up")), ((0, "qkv"),))
    for names, total in zip(last, lax.optimization_barrier([latest[names] for names in last])):
        spread(names, total)

    def to_owner(first, second):
        keep = jnp.where(on_first, first, second)
        other = lay.across_cores(jnp.where(on_first, second, first))
        return jnp.where(on_first, keep, other), jnp.where(on_first, other, keep)

    down_halves = to_owner(sums[0, "down"], sums[1, "down"])
    up_halves = to_owner(sums[0, "up"], sums[1, "up"])
    out_halves = to_owner(sums[0, "out"], sums[1, "out"])
    qkv_halves = to_owner(sums[0, "qkv"], sums[1, "qkv"])
    grad_w_down = jnp.concatenate(down_halves, axis=1).T[None]
    grad_w_up = jnp.concatenate(up_halves, axis=1)[None]
    grad_w_qkv = jnp.stack(
        [half.reshape(-1, 3, part) for half in qkv_halves], axis=2
    ).reshape(1, lay.block, 3, heads_wide)
    grad_w_out = jnp.concatenate(out_halves, axis=1).T[None]

    share = lay.block // lay.replicas
    model = lax.dynamic_slice_in_dim(summed[:6, : lay.block], replica * share, share, 1)
    vectors = [model[i : i + 1] for i in range(6)]
    parts = summed[6:8, : 3 * part].reshape(2, 3, part)
    parts = jnp.stack([parts[:, 0], parts[:, 2]]).reshape(2, 2 * part)
    grad_b_qkv = lax.dynamic_slice_in_dim(parts, replica * share, share, 1)[None]
    share_up = 2 * ff_part // lay.replicas
    ups = summed[8:10, :ff_part].reshape(1, 2 * ff_part)
    grad_b_up = lax.dynamic_slice_in_dim(ups, replica * share_up, share_up, 1)

    keep = jnp.where(on_first, back, ahead)
    other = lay.across_cores(jnp.where(on_first, ahead, back))
    boundary_out = jnp.stack([jnp.where(on_first, keep, other), jnp.where(on_first, other, keep)])
    boundary_out = boundary_out[None, :, None]
    return (
        boundary_out,
        grad_w_qkv,
        grad_b_qkv,
        grad_w_out,
        vectors[0],
        grad_w_up,
        grad_b_up,
        grad_w_down,
        vectors[1],
        vectors[2],
        vectors[3],
        vectors[4],
        vectors[5],
    )


def solution(mesh):
    spread = P("section", ("shard", "replica"))
    return jax.shard_map(
        shards,
        mesh=mesh,
        in_specs=(
            P("section", None, ("shard", "replica"), None, None),
            P(),
            P("section", None, None, "shard"),
            P("section", None, "shard"),
            P("section", "shard", None),
            P("section", None),
            P("section", None, "shard"),
            P("section", "shard"),
            P("section", "shard", None),
            P("section", None),
            P("section", None),
            P("section", None),
            P("section", None),
            P("section", None),
        ),
        out_specs=(
            P("section", None, ("shard", "replica"), None, None),
            P("section", "replica", None, "shard"),
            P("section", None, ("shard", "replica")),
            P("section", "shard", "replica"),
            spread,
            P("section", "replica", "shard"),
            spread,
            P("section", "shard", "replica"),
            spread,
            spread,
            spread,
            spread,
            spread,
        ),
        check_vma=False,
    )
```

profile of v0, /device:TPU:0, one launch (start us, length us, event | category | flops | bytes accessed | tf_op | source)
XLA Modules:
  0.0 652.5 jit_solution(14970656221350474915)
XLA Ops:
  36.7 6.5 arrange_attention.1
  44.5 12.1 %all-gather.9.cloned.1.call-done = bf16[1024,512]{1,0:T(8,128)(2,1)} async-done(((bf16[256,512]{1,0:T(8,128)(2,1)}), bf16[1024,512]{1,0:T(8,128)(2,1)}) %all-gather.9.cloned.1.call-update) | async-done | bytes 1048592 | tf_op jit(solution)/shard_map/all_gather | solution.py:371
  62.6 9.9 %collective-permute-done.4.refs_1_ = bf16[1,3,256,512]{3,2,1,0:T(8,128)(2,1)S(1)} collective-permute-done((bf16[1,3,256,512]{3,2,1,0:T(8,128)(2,1)}, bf16[1,3,256,512]{3,2,1,0:T(8,128)(2,1)S(1)}, u32[]{:S(2)}, u32[]{:S(2)}) %collective-permute-start.4) | collective-permute-done | bytes 786464 | tf_op jit(solution)/shard_map/ppermute | solution.py:125
  81.3 25.1 %all-gather.11.cloned.1.call-done = bf16[1024,1024]{1,0:T(8,128)(2,1)} async-done(((bf16[256,1024]{1,0:T(8,128)(2,1)}), bf16[1024,1024]{1,0:T(8,128)(2,1)}) %all-gather.11.cloned.1.call-update) | async-done | bytes 2097168 | tf_op jit(solution)/shard_map/all_gather | solution.py:371
  118.7 24.3 %attention_forward.2 = (bf16[592,1024]{1,0:T(8,128)(2,1)}, bf16[8,592,384]{2,1,0:T(8,128)(2,1)}, bf16[8,592,128]{2,1,0:T(8,128)(2,1)S(1)}, f32[8,8,592]{2,1,0:T(...) custom-call(bf16[2,4,256,512]{3,2,1,0:T(8,128)(2,1)S(1)} %get-tuple-element.201.refs_0_, ...), custom_call_target="tpu_custom_call" | custom-call | flops 1000 | bytes 262144 | tf_op jit(solution)/shard_map/attention_forward/pallas_call | solution.py:61
  160.1 7.1 %arrange_dense.1 = (bf16[2,4,256,1024]{3,2,1,0:T(8,128)(2,1)S(1)}, bf16[2,4,256,1024]{3,2,1,0:T(8,128)(2,1)S(1)}, f32[8,128]{1,0:T(8,128)S(1)}) custom-call(s32[7]{0:T(128)S(1)} %pad_add_fusion.refs_0_, bf16[1024,1024]{1,0:T(8,128)(2,1)} %bitcast.6.refs_3_.refs_1_, bf16[1024,1024]{1,0:T(8,128)(2,1)} %collective-permute-done.13.refs_2_, ...), custom_call_target="tpu_custom_call" | custom-call | flops 1000 | bytes 262144 | tf_op jit(solution)/shard_map/arrange_dense/pallas_call | solution.py:61
  171.2 11.5 %all-gather.15.cloned.1.call-done = bf16[1024,1024]{1,0:T(8,128)(2,1)} async-done(((bf16[256,1024]{1,0:T(8,128)(2,1)}), bf16[1024,1024]{1,0:T(8,128)(2,1)}) %all-gather.15.cloned.1.call-update) | async-done | bytes 2097168 | tf_op jit(solution)/shard_map/all_gather | solution.py:371
  186.6 9.3 %collective-permute-done.19.refs_2_ = bf16[2,3,256,1024]{3,2,1,0:T(8,128)(2,1)} collective-permute-done((bf16[2,3,256,1024]{3,2,1,0:T(8,128)(2,1)S(1)}, bf16[2,3,256,1024]{3,2,1,0:T(8,128)(2,1)}, u32[]{:S(2)}, u32[]{:S(2)}) %collective-permute-start.19) | collective-permute-done | bytes 3145760 | tf_op jit(solution)/shard_map/ppermute | solution.py:125
  200.2 7.0 %collective-permute-done.21.refs_4_ = bf16[2,3,256,1024]{3,2,1,0:T(8,128)(2,1)S(1)} collective-permute-done((bf16[2,3,256,1024]{3,2,1,0:T(8,128)(2,1)}, bf16[2,3,256,1024]{3,2,1,0:T(8,128)(2,1)S(1)}, u32[]{:S(2)}, u32[]{:S(2)}) %collective-permute-start.21) | collective-permute-done | bytes 3145760 | tf_op jit(solution)/shard_map/ppermute | solution.py:108
  208.8 18.5 %dense_forward.2 = (bf16[5,592,512]{2,1,0:T(8,128)(2,1)S(1)}, bf16[5,592,512]{2,1,0:T(8,128)(2,1)}, bf16[8,592,512]{2,1,0:T(8,128)(2,1)}, bf16[592,1024]{1,0:T(8,128)(2,1)S(1)}, f32[8,128]{1,0:T(8,128)S(1)}) custom-call(bf16[2,4,256,1024]{3,2,1,0:T(8,128)(2,1)} %copy-done, bf16[2,3,256,1024]{3,2,1,0:T(8,128)(2,1)} %copy-done.2, ...), custom_call_target="tpu_custom_call" | custom-call | flops 1000 | bytes 262144 | tf_op jit(solution)/shard_map/dense_forward/pallas_call | solution.py:61
  230.0 5.9 collective-permute-done.25.refs_4_
  235.9 24.1 %attention_forward.3 = (bf16[592,1024]{1,0:T(8,128)(2,1)}, bf16[8,592,384]{2,1,0:T(8,128)(2,1)}, bf16[8,592,128]{2,1,0:T(8,128)(2,1)S(1)}, f32[8,8,592]{2,1,0:T(...) custom-call(bf16[2,4,256,512]{3,2,1,0:T(8,128)(2,1)S(1)} %copy-done.8, ...), custom_call_target="tpu_custom_call" | custom-call | flops 1000 | bytes 262144 | tf_op jit(solution)/shard_map/attention_forward/pallas_call | solution.py:61
  260.1 4.9 collective-permute-done.27.refs_2_
  272.3 17.3 %dense_forward.3 = (bf16[5,592,512]{2,1,0:T(8,128)(2,1)S(1)}, bf16[5,592,512]{2,1,0:T(8,128)(2,1)}, bf16[8,592,512]{2,1,0:T(8,128)(2,1)}, bf16[592,1024]{1,0:T(8,128)(2,1)S(1)}, f32[8,128]{1,0:T(8,128)S(1)}) custom-call(bf16[2,4,256,1024]{3,2,1,0:T(8,128)(2,1)} %copy-done.1, bf16[2,3,256,1024]{3,2,1,0:T(8,128)(2,1)} %copy-done.3, ...), custom_call_target="tpu_custom_call" | custom-call | flops 1000 | bytes 262144 | tf_op jit(solution)/shard_map/dense_forward/pallas_call | solution.py:61
  290.2 6.5 collective-permute-done.31.refs_2_
  297.2 9.6 %weight_grads.8 = (bf16[2,4,256,512]{3,2,1,0:T(8,128)(2,1)}, bf16[2,4,256,512]{3,2,1,0:T(8,128)(2,1)S(1)}, f32[8,128]{1,0:T(8,128)S(1)}) custom-call(s32[4]{0:T(128)S(1)} %iota_xor_fusion.refs_0_, bf16[592,1024]{1,0:T(8,128)(2,1)S(1)} %copy-done.15, bf16[592,1024]{1,0:T(8,128)(2,1)S(1)} %collective-permute-done.31.refs_2_, ...), custom_call_target="tpu_custom_call" | custom-call | flops 1000 | bytes 262144 | tf_op jit(solution)/shard_map/weight_grads/pallas_call | solution.py:61
  307.2 21.1 %dense_backward.2 = (bf16[5,592,512]{2,1,0:T(8,128)(2,1)}, bf16[5,592,512]{2,1,0:T(8,128)(2,1)}, f32[8,1,512]{2,1,0:T(1,128)S(1)}, f32[592,1024]{1,0:T(8,128)S(1...) custom-call(bf16[2,4,256,1024]{3,2,1,0:T(8,128)(2,1)} %copy-done.1, ...), custom_call_target="tpu_custom_call" | custom-call | flops 1000 | bytes 262144 | tf_op jit(solution)/shard_map/dense_backward/pallas_call | solution.py:61
  336.5 5.4 weight_grads.9
  342.0 9.5 %weight_grads.10 = (bf16[2,4,256,512]{3,2,1,0:T(8,128)(2,1)}, bf16[2,4,256,512]{3,2,1,0:T(8,128)(2,1)S(1)}, f32[8,128]{1,0:T(8,128)S(1)}) custom-call(s32[4]{0:T(128)S(1)} %iota_xor_fusion.refs_0_, bf16[592,1024]{1,0:T(8,128)(2,1)S(1)} %get-tuple-element.257.refs_6_.refs_1_, bf16[592,1024]{1,0:T(8,128)(2,1)S(1)} %collective-permute-done.33.refs_2_, ...), custom_call_target="tpu_custom_call" | custom-call | flops 1000 | bytes 262144 | tf_op jit(solution)/shard_map/weight_grads/pallas_call | solution.py:61
  354.8 33.5 %attention_backward.2 = (bf16[5,592,384]{2,1,0:T(8,128)(2,1)}, bf16[5,592,384]{2,1,0:T(8,128)(2,1)}, f32[8,1,384]{2,1,0:T(1,128)S(1)}, bf16[592,1024]{1,0:T(8,12...) custom-call(bf16[2,4,256,512]{3,2,1,0:T(8,128)(2,1)} %copy-done.7, ...), custom_call_target="tpu_custom_call" | custom-call | flops 1000 | bytes 262144 | tf_op jit(solution)/shard_map/attention_backward/pallas_call | solution.py:61
  396.8 11.0 %weight_grads.11 = (bf16[2,4,256,512]{3,2,1,0:T(8,128)(2,1)}, bf16[2,4,256,512]{3,2,1,0:T(8,128)(2,1)S(1)}, f32[8,128]{1,0:T(8,128)S(1)}) custom-call(s32[4]{0:T(128)S(1)} %iota_xor_fusion.refs_0_, bf16[592,1024]{1,0:T(8,128)(2,1)S(1)} %get-tuple-element.278.refs_1_.refs_6_, bf16[592,1024]{1,0:T(8,128)(2,1)} %collective-permute-done.40.refs_2_, ...), custom_call_target="tpu_custom_call" | custom-call | flops 1000 | bytes 262144 | tf_op jit(solution)/shard_map/weight_grads/pallas_call | solution.py:61
  412.8 10.5 %weight_grads.12 = (bf16[2,4,256,384]{3,2,1,0:T(8,128)(2,1)}, bf16[2,4,256,384]{3,2,1,0:T(8,128)(2,1)S(1)}, f32[8,128]{1,0:T(8,128)S(1)}) custom-call(s32[4]{0:T(128)S(1)} %iota_xor_fusion.refs_0_, bf16[592,1024]{1,0:T(8,128)(2,1)} %get-tuple-element.279.refs_1_, bf16[592,1024]{1,0:T(8,128)(2,1)} %collective-permute-done.38.refs_2_, ...), custom_call_target="tpu_custom_call" | custom-call | flops 1000 | bytes 262144 | tf_op jit(solution)/shard_map/weight_grads/pallas_call | solution.py:61
  424.9 21.6 %dense_backward.3 = (bf16[5,592,512]{2,1,0:T(8,128)(2,1)}, bf16[5,592,512]{2,1,0:T(8,128)(2,1)}, f32[8,1,512]{2,1,0:T(1,128)S(1)}, f32[592,1024]{1,0:T(8,128)S(1...) custom-call(bf16[2,4,256,1024]{3,2,1,0:T(8,128)(2,1)} %copy-done, ...), custom_call_target="tpu_custom_call" | custom-call | flops 1000 | bytes 262144 | tf_op jit(solution)/shard_map/dense_backward/pallas_call | solution.py:61
  456.7 6.2 weight_grads.13
  463.0 11.8 %collective-permute-done.44.refs_1_ = bf16[2,4,256,384]{3,2,1,0:T(8,128)(2,1)} collective-permute-done((bf16[2,4,256,384]{3,2,1,0:T(8,128)(2,1)}, bf16[2,4,256,384]{3,2,1,0:T(8,128)(2,1)}, u32[]{:S(2)}, u32[]{:S(2)}) %collective-permute-start.44) | collective-permute-done | bytes 1572896 | tf_op jit(solution)/shard_map/ppermute | solution.py:125
  476.8 11.1 %weight_grads.14 = (bf16[2,4,256,512]{3,2,1,0:T(8,128)(2,1)}, bf16[2,4,256,512]{3,2,1,0:T(8,128)(2,1)S(1)}, f32[8,128]{1,0:T(8,128)S(1)}) custom-call(s32[4]{0:T(128)S(1)} %iota_xor_fusion.refs_0_, bf16[592,1024]{1,0:T(8,128)(2,1)} %get-tuple-element.228.refs_6_.refs_1_, bf16[592,1024]{1,0:T(8,128)(2,1)} %collective-permute-done.17.refs_2_, ...), custom_call_target="tpu_custom_call" | custom-call | flops 1000 | bytes 262144 | tf_op jit(solution)/shard_map/weight_grads/pallas_call | solution.py:61
  494.2 4.6 all-to-all-start
  499.7 34.2 %attention_backward.3 = (bf16[5,592,384]{2,1,0:T(8,128)(2,1)}, bf16[5,592,384]{2,1,0:T(8,128)(2,1)}, f32[8,1,384]{2,1,0:T(1,128)S(1)}, bf16[592,1024]{1,0:T(8,12...) custom-call(bf16[2,4,256,512]{3,2,1,0:T(8,128)(2,1)} %copy-done.6, ...), custom_call_target="tpu_custom_call" | custom-call | flops 1000 | bytes 262144 | tf_op jit(solution)/shard_map/attention_backward/pallas_call | solution.py:61
  544.4 13.3 %reduce-scatter.6.cloned.1.call-done = bf16[1,256,640]{2,1,0:T(8,128)(2,1)} async-done(((bf16[4,256,640]{2,1,0:T(8,128)(2,1)}), bf16[1,256,640]{2,1,0:T(8,128)(2,1)}) %reduce-scatter.6.cloned.1.call-update) | async-done | bytes 327696 | tf_op jit(solution)/shard_map/reduce_scatter | solution.py:1112
  557.6 5.2 all-to-all-done
  567.3 10.5 %weight_grads.15 = (bf16[2,4,256,384]{3,2,1,0:T(8,128)(2,1)}, bf16[2,4,256,384]{3,2,1,0:T(8,128)(2,1)S(1)}, f32[8,128]{1,0:T(8,128)S(1)}) custom-call(s32[4]{0:T(128)S(1)} %iota_xor_fusion.refs_0_, bf16[592,1024]{1,0:T(8,128)(2,1)} %get-tuple-element.227.refs_1_, bf16[592,1024]{1,0:T(8,128)(2,1)} %collective-permute-done.16.refs_2_, ...), custom_call_target="tpu_custom_call" | custom-call | flops 1000 | bytes 262144 | tf_op jit(solution)/shard_map/weight_grads/pallas_call | solution.py:61
  625.5 11.7 %all-to-all-done.1 = bf16[4,256,384]{2,1,0:T(8,128)(2,1)S(1)} async-done(((bf16[4,256,384]{2,1,0:T(8,128)(2,1)}), bf16[4,256,384]{2,1,0:T(8,128)(2,1)S(1)}, u32[]{:S(2)}, u32[]{:S(2)}) %all-to-all-start.1) | async-done | bytes 786464 | tf_op jit(solution)/shard_map/all_to_all | solution.py:1110
  (502 shorter events, 215.2 us)
Async XLA Ops:
  7.2 49.4 %all-gather.9.cloned.1.call-start = ((), (), s32[]{:S(2)}) async-start(), calls=%async_computation.8 | async-start | bytes 1310720 | tf_op jit(solution)/shard_map/all_gather | solution.py:371
  26.2 80.2 %all-gather.11.cloned.1.call-start = ((), (), s32[]{:S(2)}) async-start(), calls=%async_computation.9 | async-start | bytes 2621440 | tf_op jit(solution)/shard_map/all_gather | solution.py:371
  60.2 92.9 %all-gather.13.cloned.1.call-start = ((), (), s32[]{:S(2)}) async-start(), calls=%async_computation.10 | async-start | bytes 1310720 | tf_op jit(solution)/shard_map/all_gather | solution.py:371
  75.0 37.1 %collective-permute-start.6 = (bf16[2,3,256,512]{3,2,1,0:T(8,128)(2,1)}, bf16[2,3,256,512]{3,2,1,0:T(8,128)(2,1)}, u32[]{:S(2)}, u32[]{:S(2)}) collective-permute-start(bf16[2,3,256,512]{3,2,1,0:T(8,128)(2,1)} %get-tuple-element.210.refs_1_), channel_id=1, source_target_pairs={{0,2},{1,3},{2,0},{3,1},{4,6},{5,7},{6,4},{7,5},{8,10},{9,11},{10,... | collective-permute-start | bytes 4718600 | tf_op jit(solution)/shard_map/ppermute | solution.py:125
  76.7 36.9 %collective-permute-start.12 = (bf16[2,1536]{1,0:T(2,128)(2,1)S(1)}, bf16[2,1536]{1,0:T(2,128)(2,1)S(1)}, u32[]{:S(2)}, u32[]{:S(2)}) collective-permute-start(bf16[2,1536]{1,0:T(2,128)(2,1)S(1)} %pad_maximum_fusion.6), channel_id=1, source_target_pairs={{0,12},{4,8},{8,4},{12,0},{1,13},{5,9},{9,5},{13,1},{2,14},{6,10},... | collective-permute-start | bytes 18440 | tf_op jit(solution)/shard_map/ppermute | solution.py:111
  80.4 38.3 %collective-permute-start.7 = (bf16[2,3,256,512]{3,2,1,0:T(8,128)(2,1)}, bf16[2,3,256,512]{3,2,1,0:T(8,128)(2,1)}, u32[]{:S(2)}, u32[]{:S(2)}) collective-permute-start(bf16[2,3,256,512]{3,2,1,0:T(8,128)(2,1)} %get-tuple-element.210.refs_1_), channel_id=1, source_target_pairs={{0,16},{16,0},{1,17},{17,1},{2,18},{18,2},{3,19},{19,3},{4,20},{20... | collective-permute-start | bytes 4718600 | tf_op jit(solution)/shard_map/ppermute | solution.py:108
  81.2 101.5 %all-gather.15.cloned.1.call-start = ((), (), s32[]{:S(2)}) async-start(), calls=%async_computation.11 | async-start | bytes 2621440 | tf_op jit(solution)/shard_map/all_gather | solution.py:371
  118.1 329.8 %reduce-scatter.4.cloned.1.call-start = ((), (), s32[]{:S(2)}) async-start(), calls=%async_computation.5 | async-start | bytes 1310720 | tf_op jit(solution)/shard_map/reduce_scatter | solution.py:1112
  145.9 49.9 %collective-permute-start.19 = (bf16[2,3,256,1024]{3,2,1,0:T(8,128)(2,1)S(1)}, bf16[2,3,256,1024]{3,2,1,0:T(8,128)(2,1)}, u32[]{:S(2)}, u32[]{:S(2)}) collective-permute-start(bf16[2,3,256,1024]{3,2,1,0:T(8,128)(2,1)S(1)} %get-tuple-element.230.refs_1_), channel_id=1, source_target_pairs={{0,2},{1,3},{2,0},{3,1},{4,6},{5,7},{6,4},{7,5},{8,10},{9,11},{10,... | collective-permute-start | bytes 9437192 | tf_op jit(solution)/shard_map/ppermute | solution.py:125
  156.4 39.5 %collective-permute-start.22 = (bf16[1,3,256,512]{3,2,1,0:T(8,128)(2,1)}, bf16[1,3,256,512]{3,2,1,0:T(8,128)(2,1)}, u32[]{:S(2)}, u32[]{:S(2)}) collective-permute-start(bf16[1,3,256,512]{3,2,1,0:T(8,128)(2,1)} %get-tuple-element.236.refs_0_), channel_id=1, source_target_pairs={{0,1},{1,0},{2,3},{3,2},{4,5},{5,4},{6,7},{7,6},{8,9},{9,8},{10,11... | collective-permute-start | bytes 2359304 | tf_op jit(solution)/shard_map/ppermute | solution.py:125
  159.3 40.8 %collective-permute-start.20 = (bf16[2,3,256,1024]{3,2,1,0:T(8,128)(2,1)S(1)}, bf16[2,3,256,1024]{3,2,1,0:T(8,128)(2,1)}, u32[]{:S(2)}, u32[]{:S(2)}) collective-permute-start(bf16[2,3,256,1024]{3,2,1,0:T(8,128)(2,1)S(1)} %get-tuple-element.230.refs_1_), channel_id=1, source_target_pairs={{0,16},{16,0},{1,17},{17,1},{2,18},{18,2},{3,19},{19,3},{4,20},{20... | collective-permute-start | bytes 9437192 | tf_op jit(solution)/shard_map/ppermute | solution.py:108
  185.0 42.3 %collective-permute-start.26 = (bf16[1,3,256,1024]{3,2,1,0:T(8,128)(2,1)S(1)}, bf16[1,3,256,1024]{3,2,1,0:T(8,128)(2,1)S(1)}, u32[]{:S(2)}, u32[]{:S(2)}) collective-permute-start(bf16[1,3,256,1024]{3,2,1,0:T(8,128)(2,1)S(1)} %get-tuple-element.246.refs_0_), channel_id=1, source_target_pairs={{0,1},{1,0},{2,3},{3,2},{4,5},{5,4},{6,7},{7,6},{8,9},{9,8},{10,11... | collective-permute-start | bytes 4718600 | tf_op jit(solution)/shard_map/ppermute | solution.py:125
  227.6 37.3 %collective-permute-start.27 = (bf16[2,3,256,1024]{3,2,1,0:T(8,128)(2,1)S(1)}, bf16[2,3,256,1024]{3,2,1,0:T(8,128)(2,1)S(1)}, u32[]{:S(2)}, u32[]{:S(2)}) collective-permute-start(bf16[2,3,256,1024]{3,2,1,0:T(8,128)(2,1)S(1)} %get-tuple-element.254.refs_1_), channel_id=1, source_target_pairs={{0,2},{1,3},{2,0},{3,1},{4,6},{5,7},{6,4},{7,5},{8,10},{9,11},{10,... | collective-permute-start | bytes 9437192 | tf_op jit(solution)/shard_map/ppermute | solution.py:125
  228.1 38.5 %collective-permute-start.28 = (bf16[2,3,256,1024]{3,2,1,0:T(8,128)(2,1)S(1)}, bf16[2,3,256,1024]{3,2,1,0:T(8,128)(2,1)}, u32[]{:S(2)}, u32[]{:S(2)}) collective-permute-start(bf16[2,3,256,1024]{3,2,1,0:T(8,128)(2,1)S(1)} %get-tuple-element.254.refs_1_), channel_id=1, source_target_pairs={{0,16},{16,0},{1,17},{17,1},{2,18},{18,2},{3,19},{19,3},{4,20},{20... | collective-permute-start | bytes 9437192 | tf_op jit(solution)/shard_map/ppermute | solution.py:108
  334.7 53.7 %collective-permute-start.43 = (bf16[1,4,256,512]{3,2,1,0:T(8,128)(2,1)}, bf16[1,4,256,512]{3,2,1,0:T(8,128)(2,1)S(1)}, u32[]{:S(2)}, u32[]{:S(2)}) collective-permute-start(bf16[1,4,256,512]{3,2,1,0:T(8,128)(2,1)} %get-tuple-element.287), channel_id=1, source_target_pairs={{0,1},{1,0},{2,3},{3,2},{4,5},{5,4},{6,7},{7,6},{8,9},{9,8},{10,11... | collective-permute-start | bytes 3145736 | tf_op jit(solution)/shard_map/ppermute | solution.py:125
  352.7 40.4 %collective-permute-start.41 = (bf16[2,4,256,512]{3,2,1,0:T(8,128)(2,1)}, bf16[2,4,256,512]{3,2,1,0:T(8,128)(2,1)}, u32[]{:S(2)}, u32[]{:S(2)}) collective-permute-start(bf16[2,4,256,512]{3,2,1,0:T(8,128)(2,1)} %get-tuple-element.284), channel_id=1, source_target_pairs={{0,2},{1,3},{2,0},{3,1},{4,6},{5,7},{6,4},{7,5},{8,10},{9,11},{10,... | collective-permute-start | bytes 6291464 | tf_op jit(solution)/shard_map/ppermute | solution.py:125
  354.3 58.5 %collective-permute-start.38 = (bf16[592,1024]{1,0:T(8,128)(2,1)}, bf16[592,1024]{1,0:T(8,128)(2,1)}, u32[]{:S(2)}, u32[]{:S(2)}) collective-permute-start(bf16[592,1024]{1,0:T(8,128)(2,1)} %get-tuple-element.279.refs_1_), channel_id=1, source_target_pairs={{0,16},{16,0},{1,17},{17,1},{2,18},{18,2},{3,19},{19,3},{4,20},{20... | collective-permute-start | bytes 3637256 | tf_op jit(solution)/shard_map/ppermute | solution.py:108
  354.3 35.9 %collective-permute-start.42 = (bf16[2,4,256,128]{3,2,1,0:T(8,128)(2,1)}, bf16[2,4,256,128]{3,2,1,0:T(8,128)(2,1)}, u32[]{:S(2)}, u32[]{:S(2)}) collective-permute-start(bf16[2,4,256,128]{3,2,1,0:T(8,128)(2,1)} %get-tuple-element.286), channel_id=1, source_target_pairs={{0,2},{1,3},{2,0},{3,1},{4,6},{5,7},{6,4},{7,5},{8,10},{9,11},{10,... | collective-permute-start | bytes 1572872 | tf_op jit(solution)/shard_map/ppermute | solution.py:125
  409.1 43.3 %collective-permute-start.46 = (bf16[2,4,256,512]{3,2,1,0:T(8,128)(2,1)}, bf16[2,4,256,512]{3,2,1,0:T(8,128)(2,1)}, u32[]{:S(2)}, u32[]{:S(2)}) collective-permute-start(bf16[2,4,256,512]{3,2,1,0:T(8,128)(2,1)} %get-tuple-element.299), channel_id=1, source_target_pairs={{0,2},{1,3},{2,0},{3,1},{4,6},{5,7},{6,4},{7,5},{8,10},{9,11},{10,... | collective-permute-start | bytes 6291464 | tf_op jit(solution)/shard_map/ppermute | solution.py:125
  410.8 37.7 %collective-permute-start.48 = (bf16[1,4,256,512]{3,2,1,0:T(8,128)(2,1)}, bf16[1,4,256,512]{3,2,1,0:T(8,128)(2,1)}, u32[]{:S(2)}, u32[]{:S(2)}) collective-permute-start(bf16[1,4,256,512]{3,2,1,0:T(8,128)(2,1)} %get-tuple-element.301), channel_id=1, source_target_pairs={{0,1},{1,0},{2,3},{3,2},{4,5},{5,4},{6,7},{7,6},{8,9},{9,8},{10,11... | collective-permute-start | bytes 3145736 | tf_op jit(solution)/shard_map/ppermute | solution.py:125
  411.1 36.9 %collective-permute-start.47 = (bf16[1,4,256,128]{3,2,1,0:T(8,128)(2,1)}, bf16[1,4,256,128]{3,2,1,0:T(8,128)(2,1)}, u32[]{:S(2)}, u32[]{:S(2)}) collective-permute-start(bf16[1,4,256,128]{3,2,1,0:T(8,128)(2,1)} %get-tuple-element.300), channel_id=1, source_target_pairs={{0,1},{1,0},{2,3},{3,2},{4,5},{5,4},{6,7},{7,6},{8,9},{9,8},{10,11... | collective-permute-start | bytes 786440 | tf_op jit(solution)/shard_map/ppermute | solution.py:125
  424.5 50.2 %collective-permute-start.44 = (bf16[2,4,256,384]{3,2,1,0:T(8,128)(2,1)}, bf16[2,4,256,384]{3,2,1,0:T(8,128)(2,1)}, u32[]{:S(2)}, u32[]{:S(2)}) collective-permute-start(bf16[2,4,256,384]{3,2,1,0:T(8,128)(2,1)} %get-tuple-element.297), channel_id=1, source_target_pairs={{0,2},{1,3},{2,0},{3,1},{4,6},{5,7},{6,4},{7,5},{8,10},{9,11},{10,... | collective-permute-start | bytes 4718600 | tf_op jit(solution)/shard_map/ppermute | solution.py:125
  455.1 35.7 %collective-permute-start.50 = (bf16[1,4,256,512]{3,2,1,0:T(8,128)(2,1)S(1)}, bf16[1,4,256,512]{3,2,1,0:T(8,128)(2,1)S(1)}, u32[]{:S(2)}, u32[]{:S(2)}) collective-permute-start(bf16[1,4,256,512]{3,2,1,0:T(8,128)(2,1)S(1)} %get-tuple-element.309), channel_id=1, source_target_pairs={{0,1},{1,0},{2,3},{3,2},{4,5},{5,4},{6,7},{7,6},{8,9},{9,8},{10,11... | collective-permute-start | bytes 3145736 | tf_op jit(solution)/shard_map/ppermute | solution.py:125
  489.3 51.1 %collective-permute-start.58 = (bf16[2,4,256,512]{3,2,1,0:T(8,128)(2,1)}, bf16[2,4,256,512]{3,2,1,0:T(8,128)(2,1)}, u32[]{:S(2)}, u32[]{:S(2)}) collective-permute-start(bf16[2,4,256,512]{3,2,1,0:T(8,128)(2,1)} %get-tuple-element.345), channel_id=1, source_target_pairs={{0,2},{1,3},{2,0},{3,1},{4,6},{5,7},{6,4},{7,5},{8,10},{9,11},{10,... | collective-permute-start | bytes 6291464 | tf_op jit(solution)/shard_map/ppermute | solution.py:125
  494.2 68.6 %all-to-all-start = ((bf16[4,256,896]{2,1,0:T(8,128)(2,1)}), bf16[4,256,896]{2,1,0:T(8,128)(2,1)}, u32[]{:S(2)}, u32[]{:S(2)}) async-start(bf16[4,256,896]{2,1,0:T(8,128)(2,1)} %bitcast.140), calls=%async_computation.2 | async-start | bytes 3670016 | tf_op jit(solution)/shard_map/all_to_all | solution.py:1110
  498.8 58.8 %reduce-scatter.6.cloned.1.call-start = ((), (), s32[]{:S(2)}) async-start(), calls=%async_computation.6 | async-start | bytes 1638400 | tf_op jit(solution)/shard_map/reduce_scatter | solution.py:1112
  498.8 36.2 %collective-permute-start.53 = (bf16[2,4,256,128]{3,2,1,0:T(8,128)(2,1)}, bf16[2,4,256,128]{3,2,1,0:T(8,128)(2,1)S(1)}, u32[]{:S(2)}, u32[]{:S(2)}) collective-permute-start(bf16[2,4,256,128]{3,2,1,0:T(8,128)(2,1)} %copy-done.76), channel_id=1, source_target_pairs={{0,2},{1,3},{2,0},{3,1},{4,6},{5,7},{6,4},{7,5},{8,10},{9,11},{10,... | collective-permute-start | bytes 1572872 | tf_op jit(solution)/shard_map/ppermute | solution.py:125
  499.5 125.9 %reduce-scatter.8.cloned.1.call-start = ((), (), s32[]{:S(2)}) async-start(), calls=%async_computation.7 | async-start | bytes 1638400 | tf_op jit(solution)/shard_map/reduce_scatter | solution.py:1112
  536.0 41.9 %collective-permute-start.54 = (f32[16,512]{1,0:T(8,128)S(1)}, f32[16,512]{1,0:T(8,128)S(1)}, u32[]{:S(2)}, u32[]{:S(2)}) collective-permute-start(f32[16,512]{1,0:T(8,128)S(1)} %get-tuple-element.451), channel_id=1, source_target_pairs={{0,4},{4,0},{8,12},{12,8},{1,5},{5,1},{9,13},{13,9},{2,6},{6,2},{1... | collective-permute-start | bytes 98312 | tf_op jit(solution)/shard_map/ppermute | solution.py:111
  537.9 40.0 %collective-permute-start.55 = (f32[16,512]{1,0:T(8,128)S(1)}, f32[16,512]{1,0:T(8,128)S(1)}, u32[]{:S(2)}, u32[]{:S(2)}) collective-permute-start(f32[16,512]{1,0:T(8,128)S(1)} %get-tuple-element.450), channel_id=1, source_target_pairs={{0,8},{4,12},{8,0},{12,4},{1,9},{5,13},{9,1},{13,5},{2,10},{6,14},... | collective-permute-start | bytes 98312 | tf_op jit(solution)/shard_map/ppermute | solution.py:111
  540.3 37.6 %collective-permute-start.56 = (f32[16,512]{1,0:T(8,128)S(1)}, f32[16,512]{1,0:T(8,128)S(1)}, u32[]{:S(2)}, u32[]{:S(2)}) collective-permute-start(f32[16,512]{1,0:T(8,128)S(1)} %get-tuple-element.449), channel_id=1, source_target_pairs={{0,12},{4,8},{8,4},{12,0},{1,13},{5,9},{9,5},{13,1},{2,14},{6,10},... | collective-permute-start | bytes 98312 | tf_op jit(solution)/shard_map/ppermute | solution.py:111
  542.9 45.5 %collective-permute-start.61 = (bf16[1,4,256,512]{3,2,1,0:T(8,128)(2,1)}, bf16[1,4,256,512]{3,2,1,0:T(8,128)(2,1)}, u32[]{:S(2)}, u32[]{:S(2)}) collective-permute-start(bf16[1,4,256,512]{3,2,1,0:T(8,128)(2,1)} %get-tuple-element.359), channel_id=1, source_target_pairs={{0,1},{1,0},{2,3},{3,2},{4,5},{5,4},{6,7},{7,6},{8,9},{9,8},{10,11... | collective-permute-start | bytes 3145736 | tf_op jit(solution)/shard_map/ppermute | solution.py:125
  (149 other events, 1615.7 us)
Sparse Core Ops, SparseCore 0:
  26.3 30.2 all-gather.8
  60.3 45.9 all-gather.10
  108.5 26.6 all-gather.12
  137.2 45.4 all-gather.14
  390.4 24.6 reduce-scatter.3
  501.7 55.8 reduce-scatter.5
  591.7 28.9 reduce-scatter.7
where the time goes:
time: 661 us; the launch traced here: 653 us
  Pallas kernels  326 us (49%)
  waiting for transfers between devices  165 us (25%)
  local copies, waits for them, and re-layouts  72.6 us (11%)
  starting transfers between devices  52.9 us (8%)
  other arithmetic  20 us (3%)
  between operations  16.5 us (2%)
    pallas_call x51, Pallas kernels, launch(): pl.pallas_call(ordered, grid_spec=pltpu.PrefetchScalarGridSpec(num_scalar...  326 us
    unnamed x220, local copies, waits for them, and re-layouts  58.2 us
    all_gather x4, waiting for transfers between devices, start(): self.state[n] = lax.all_gather(piece, 'shard')  48.7 us
    ppermute x24, waiting for transfers between devices, along_bit(): return lax.ppermute(value, ALL_AXES, route)  47.4 us
    ppermute x38, waiting for transfers between devices, across_cores(): return lax.ppermute(value, 'section', [(0, 1), (1, 0)])  34.9 us
    ppermute x24, starting transfers between devices, along_bit(): return lax.ppermute(value, ALL_AXES, route)  25.2 us
    all_to_all x2, waiting for transfers between devices, collect(): latest[names] = lax.all_to_all(total, 'shard', 0, 0, tiled=True)  16.8 us
    reduce_scatter x3, waiting for transfers between devices, collect(): latest[names] = lax.psum_scatter(total, 'shard', scatter_dimension=0)[None]  13.3 us
  transfers between devices with their start and end apart: 79, of which 24 were waited for; matrix products, arithmetic and copies ran while one was open for 5% of the time, Pallas kernels for 45%

commit v1 on v0

--- a/solution.py
+++ b/solution.py
@@ -824,29 +824,19 @@
         feature_spec = pl.BlockSpec((1, PAD, feats.shape[2]), lambda k, s: (k, 0, 0))
         specs += [whole, whole, feature_spec, feature_spec]
         operands += [x, x_other, feats, feats_other]
-        scratch += [pltpu.VMEM((width, PAD), LOW)] * 2
 
     def kernel(_, *refs):
-        far_ref, near_ref = refs[4 * len(pairs) : 4 * len(pairs) + 2]
-        turned = refs[4 * len(pairs) + 2 :]
-
-        @pl.when(pl.program_id(0) == 0)
-        def _():
-            for n in range(len(pairs)):
-                for b in range(lay.replicas):
-                    rows = slice(b * block, (b + 1) * block)
-                    other = slice(lay.flip[b] * block, (lay.flip[b] + 1) * block)
-                    turned[2 * n][rows, :] = refs[4 * n][:, rows].T
-                    turned[2 * n + 1][rows, :] = refs[4 * n + 1][:, other].T
-
+        far_ref, near_ref = refs[4 * len(pairs) :]
         start = 0
         for n, size in enumerate(sizes):
-            grads = product(turned[2 * n][...], refs[4 * n + 2][0], NN) + product(
-                turned[2 * n + 1][...], refs[4 * n + 3][0], NN
-            )
-            grads = grads.reshape(2 * half, block, size).astype(LOW)
-            near_ref[:, 0, :, start : start + size] = grads[:half]
-            far_ref[:, 0, :, start : start + size] = grads[half:]
+            x, x_other, feats, feats_other = refs[4 * n : 4 * n + 4]
+            for b in range(2 * half):
+                mine = slice(b * block, (b + 1) * block)
+                other = slice(lay.flip[b] * block, (lay.flip[b] + 1) * block)
+                grads = product(x[:, mine], feats[0], TN)
+                grads = (grads + product(x_other[:, other], feats_other[0], TN)).astype(LOW)
+                ref = near_ref if b < half else far_ref
+                ref[b % half, 0, :, start : start + size] = grads
             start += size
 
     return launch(
@@ -1104,12 +1094,15 @@
             sent = add_blocks(lay, group, cost=cost)
             terms[name] = terms[name] + [(lay.along_bit(sent, bit), 0)]
 
-    def collect(names, direct, cost=10**10):
+    def collect(names, direct, cost=10**10, beside=None):
         total = add_blocks(lay, *(terms[name] for name in names), cost=cost)[0]
+        if beside is not None:
+            total, beside = lax.optimization_barrier((total, beside))
         if direct:
             latest[names] = lax.all_to_all(total, "shard", 0, 0, tiled=True)
         else:
             latest[names] = lax.psum_scatter(total, "shard", scatter_dimension=0)[None]
+        return beside
 
     def settle(*all_names):
         for names, total in zip(all_names, lay.hold(*(latest[names] for names in all_names))):
@@ -1170,7 +1163,8 @@
             )
         )
         tangent = grad_entry
-        mixed_other = lay.across_cores(mixed_sent)
+        if layer == 1:
+            mixed_other = lay.across_cores(mixed_sent)
         vector_sums[layer] = (
             [out_sums, down_sums, gain_one_sum, shift_one_sum, gain_two_sum, shift_two_sum],
             up_sums,
@@ -1185,28 +1179,31 @@
         if layer == 0:
             (send,) = lay.hold(send)
             summed = keep + send
-            coming = [lay.along_shard(summed[k], k) for k in range(1, lay.shards)]
+        if layer == 0:
+            (mixed_sent,) = lay.hold(mixed_sent)
+            mixed_other = lay.across_cores(mixed_sent)
         halve((layer, "up"))
-        if layer == 0:
-            settle(((1, "out"), (1, "up")), ((1, "qkv"), (0, "down")))
-            pause(lay, 10**10)
         if layer == 1:
             active, active_other = kept[0][7], kept[0][9][3]
             begin((0, "down"), (tangent, lay.across_cores(tangent), active, active_other))
         begin((layer, "qkv"), (normed, normed_other, grad_mixed, mixed_other))
-    summed = sum(lay.hold(*coming), summed[0])
+    (summed,) = lay.hold(summed)
     coming = lay.along_bit_plain(summed, 0)
+    settle(((1, "out"), (1, "up")))
     back = restore_image(lay, tangent, blocks, jnp.ones((1,), F32))
     ahead = restore_image(lay, entry, blocks, live)
+    (coming,) = lay.hold(coming)
+    for bit in range(1, lay.bits):
+        summed = summed + coming
+        coming = lay.along_bit_plain(summed, bit)
     collect(((0, "out"), (0, "up")), False, cost=2 * 10**10)
     halve((0, "qkv"), cost=1000)
-    back, ahead = lay.hold(back, ahead)
-    for bit in range(lay.bits):
-        (coming,) = lay.hold(coming)
-        summed = summed + coming
-        if bit + 1 < lay.bits:
-            coming = lay.along_bit_plain(summed, bit + 1)
-    collect(((0, "qkv"),), True, cost=1000)
+    settle(((1, "qkv"), (0, "down")))
+    back, ahead, coming = lay.hold(back, ahead, coming)
+    summed = summed + coming
+    coming = [lay.along_shard(summed[k], k) for k in range(1, lay.shards)]
+    coming = collect(((0, "qkv"),), True, cost=1000, beside=coming)
+    summed = sum(coming, summed[0])
     last = (((0, "out"), (0, "up")), ((0, "qkv"),))
     for names, total in zip(last, lax.optimization_barrier([latest[names] for names in last])):
         spread(names, total)

time: 661 us -> 651 us (0.985)
  waiting for transfers between devices: 165 us -> 154 us
    reduce_scatter x3, waiting for transfers between devices: 13.3 us -> 0.01 us  [collect(): latest[names] = lax.psum_scatter(total, 'shard', scatter_dimension=0)[None]]
    unnamed x220 -> x236, local copies, waits for them, and re-layouts: 58.2 us -> 64 us
    pallas_call x51 -> x50, Pallas kernels: 326 us -> 321 us  [launch(): pl.pallas_call(ordered, grid_spec=pltpu.PrefetchScalarGridSpec(num_scalar...]
where the time goes in v1:
time: 651 us; the launch traced here: 642 us
  Pallas kernels  321 us (49%)
  waiting for transfers between devices  154 us (24%)
  local copies, waits for them, and re-layouts  79 us (12%)
  starting transfers between devices  53.1 us (8%)
  other arithmetic  19.1 us (3%)
  between operations  16.6 us (3%)
    pallas_call x50, Pallas kernels, launch(): pl.pallas_call(ordered, grid_spec=pltpu.PrefetchScalarGridSpec(num_scalar...  321 us
    unnamed x236, local copies, waits for them, and re-layouts  64 us
    ppermute x24, waiting for transfers between devices, along_bit(): return lax.ppermute(value, ALL_AXES, route)  52.7 us
    all_gather x4, waiting for transfers between devices, start(): self.state[n] = lax.all_gather(piece, 'shard')  48.6 us
    ppermute x38, waiting for transfers between devices, across_cores(): return lax.ppermute(value, 'section', [(0, 1), (1, 0)])  35.1 us
    ppermute x24, starting transfers between devices, along_bit(): return lax.ppermute(value, ALL_AXES, route)  27.7 us
    all_to_all x2, waiting for transfers between devices, collect(): latest[names] = lax.all_to_all(total, 'shard', 0, 0, tiled=True)  13.5 us
  transfers between devices with their start and end apart: 79, of which 24 were waited for; matrix products, arithmetic and copies ran while one was open for 5% of the time, Pallas kernels for 45%

profile of v1, /device:TPU:0, one launch (start us, length us, event | category | flops | bytes accessed | tf_op | source)
XLA Modules:
  0.0 642.5 jit_solution(14550864849777273020)
XLA Ops:
  36.7 6.5 %arrange_attention.1 = (bf16[2,4,256,512]{3,2,1,0:T(8,128)(2,1)S(1)}, bf16[2,4,256,512]{3,2,1,0:T(8,128)(2,1)S(1)}, f32[8,128]{1,0:T(8,128)S(1)}) custom-call(s32[7]{0:T(128)S(1)} %pad_add_fusion.refs_0_, bf16[1024,768]{1,0:T(8,128)(2,1)} %copy.68.refs_1_, bf16[1024,768]{1,0:T(8,128)(2,1)} %collective-permute-done.refs_2_, bf16[256,1024]{1,0:T(8,128)(2,1)S(1)} %bitcast.137, ...), custom_call_target="tpu_custom_call" | custom-call | flops 1000 | bytes 262144 | tf_op jit(solution)/shard_map/arrange_attention/pallas_call | solution.py:61
  44.5 12.0 %all-gather.9.cloned.1.call-done = bf16[1024,512]{1,0:T(8,128)(2,1)} async-done(((bf16[256,512]{1,0:T(8,128)(2,1)}), bf16[1024,512]{1,0:T(8,128)(2,1)}) %all-gather.9.cloned.1.call-update) | async-done | bytes 1048592 | tf_op jit(solution)/shard_map/all_gather | solution.py:371
  62.6 9.9 %collective-permute-done.4.refs_1_ = bf16[1,3,256,512]{3,2,1,0:T(8,128)(2,1)S(1)} collective-permute-done((bf16[1,3,256,512]{3,2,1,0:T(8,128)(2,1)}, bf16[1,3,256,512]{3,2,1,0:T(8,128)(2,1)S(1)}, u32[]{:S(2)}, u32[]{:S(2)}) %collective-permute-start.4) | collective-permute-done | bytes 786464 | tf_op jit(solution)/shard_map/ppermute | solution.py:125
  81.2 25.1 %all-gather.11.cloned.1.call-done = bf16[1024,1024]{1,0:T(8,128)(2,1)} async-done(((bf16[256,1024]{1,0:T(8,128)(2,1)}), bf16[1024,1024]{1,0:T(8,128)(2,1)}) %all-gather.11.cloned.1.call-update) | async-done | bytes 2097168 | tf_op jit(solution)/shard_map/all_gather | solution.py:371
  118.7 24.4 %attention_forward.2 = (bf16[592,1024]{1,0:T(8,128)(2,1)}, bf16[8,592,384]{2,1,0:T(8,128)(2,1)}, bf16[8,592,128]{2,1,0:T(8,128)(2,1)S(1)}, f32[8,8,592]{2,1,0:T(...) custom-call(bf16[2,4,256,512]{3,2,1,0:T(8,128)(2,1)S(1)} %get-tuple-element.204.refs_0_, ...), custom_call_target="tpu_custom_call" | custom-call | flops 1000 | bytes 262144 | tf_op jit(solution)/shard_map/attention_forward/pallas_call | solution.py:61
  160.2 7.1 %arrange_dense.1 = (bf16[2,4,256,1024]{3,2,1,0:T(8,128)(2,1)S(1)}, bf16[2,4,256,1024]{3,2,1,0:T(8,128)(2,1)S(1)}, f32[8,128]{1,0:T(8,128)S(1)}) custom-call(s32[7]{0:T(128)S(1)} %pad_add_fusion.refs_0_, bf16[1024,1024]{1,0:T(8,128)(2,1)} %bitcast.6.refs_3_.refs_1_, bf16[1024,1024]{1,0:T(8,128)(2,1)} %collective-permute-done.13.refs_2_, ...), custom_call_target="tpu_custom_call" | custom-call | flops 1000 | bytes 262144 | tf_op jit(solution)/shard_map/arrange_dense/pallas_call | solution.py:61
  171.2 11.5 %all-gather.15.cloned.1.call-done = bf16[1024,1024]{1,0:T(8,128)(2,1)} async-done(((bf16[256,1024]{1,0:T(8,128)(2,1)}), bf16[1024,1024]{1,0:T(8,128)(2,1)}) %all-gather.15.cloned.1.call-update) | async-done | bytes 2097168 | tf_op jit(solution)/shard_map/all_gather | solution.py:371
  186.5 9.3 %collective-permute-done.19.refs_2_ = bf16[2,3,256,1024]{3,2,1,0:T(8,128)(2,1)} collective-permute-done((bf16[2,3,256,1024]{3,2,1,0:T(8,128)(2,1)S(1)}, bf16[2,3,256,1024]{3,2,1,0:T(8,128)(2,1)}, u32[]{:S(2)}, u32[]{:S(2)}) %collective-permute-start.19) | collective-permute-done | bytes 3145760 | tf_op jit(solution)/shard_map/ppermute | solution.py:125
  200.2 7.0 %collective-permute-done.21.refs_4_ = bf16[2,3,256,1024]{3,2,1,0:T(8,128)(2,1)S(1)} collective-permute-done((bf16[2,3,256,1024]{3,2,1,0:T(8,128)(2,1)}, bf16[2,3,256,1024]{3,2,1,0:T(8,128)(2,1)S(1)}, u32[]{:S(2)}, u32[]{:S(2)}) %collective-permute-start.21) | collective-permute-done | bytes 3145760 | tf_op jit(solution)/shard_map/ppermute | solution.py:108
  208.8 18.5 %dense_forward.2 = (bf16[5,592,512]{2,1,0:T(8,128)(2,1)S(1)}, bf16[5,592,512]{2,1,0:T(8,128)(2,1)}, bf16[8,592,512]{2,1,0:T(8,128)(2,1)}, bf16[592,1024]{1,0:T(8,128)(2,1)S(1)}, f32[8,128]{1,0:T(8,128)S(1)}) custom-call(bf16[2,4,256,1024]{3,2,1,0:T(8,128)(2,1)} %copy-done, bf16[2,3,256,1024]{3,2,1,0:T(8,128)(2,1)} %copy-done.2, ...), custom_call_target="tpu_custom_call" | custom-call | flops 1000 | bytes 262144 | tf_op jit(solution)/shard_map/dense_forward/pallas_call | solution.py:61
  230.1 5.8 collective-permute-done.25.refs_4_
  236.0 24.1 %attention_forward.3 = (bf16[592,1024]{1,0:T(8,128)(2,1)}, bf16[8,592,384]{2,1,0:T(8,128)(2,1)}, bf16[8,592,128]{2,1,0:T(8,128)(2,1)S(1)}, f32[8,8,592]{2,1,0:T(...) custom-call(bf16[2,4,256,512]{3,2,1,0:T(8,128)(2,1)S(1)} %copy-done.8, ...), custom_call_target="tpu_custom_call" | custom-call | flops 1000 | bytes 262144 | tf_op jit(solution)/shard_map/attention_forward/pallas_call | solution.py:61
  260.2 4.9 collective-permute-done.27.refs_2_
  272.4 17.3 %dense_forward.3 = (bf16[5,592,512]{2,1,0:T(8,128)(2,1)S(1)}, bf16[5,592,512]{2,1,0:T(8,128)(2,1)}, bf16[8,592,512]{2,1,0:T(8,128)(2,1)}, bf16[592,1024]{1,0:T(8,128)(2,1)S(1)}, f32[8,128]{1,0:T(8,128)S(1)}) custom-call(bf16[2,4,256,1024]{3,2,1,0:T(8,128)(2,1)} %copy-done.1, bf16[2,3,256,1024]{3,2,1,0:T(8,128)(2,1)} %copy-done.3, ...), custom_call_target="tpu_custom_call" | custom-call | flops 1000 | bytes 262144 | tf_op jit(solution)/shard_map/dense_forward/pallas_call | solution.py:61
  290.3 6.5 %collective-permute-done.31.refs_2_ = bf16[592,1024]{1,0:T(8,128)(2,1)S(1)} collective-permute-done((bf16[592,1024]{1,0:T(8,128)(2,1)S(1)}, bf16[592,1024]{1,0:T(8,128)(2,1)S(1)}, u32[]{:S(2)}, u32[]{:S(2)}) %collective-permute-start.31) | collective-permute-done | bytes 1212448 | tf_op jit(solution)/shard_map/ppermute | solution.py:108
  297.2 9.0 %weight_grads.8 = (bf16[2,4,256,512]{3,2,1,0:T(8,128)(2,1)}, bf16[2,4,256,512]{3,2,1,0:T(8,128)(2,1)S(1)}, f32[8,128]{1,0:T(8,128)S(1)}) custom-call(s32[4]{0:T(128)S(1)} %iota_xor_fusion.refs_0_, bf16[592,1024]{1,0:T(8,128)(2,1)S(1)} %copy-done.15, bf16[592,1024]{1,0:T(8,128)(2,1)S(1)} %collective-permute-done.31.refs_2_, ...), custom_call_target="tpu_custom_call" | custom-call | flops 1000 | bytes 262144 | tf_op jit(solution)/shard_map/weight_grads/pallas_call | solution.py:61
  306.7 21.2 %dense_backward.2 = (bf16[5,592,512]{2,1,0:T(8,128)(2,1)}, bf16[5,592,512]{2,1,0:T(8,128)(2,1)}, f32[8,1,512]{2,1,0:T(1,128)S(1)}, f32[592,1024]{1,0:T(8,128)S(1...) custom-call(bf16[2,4,256,1024]{3,2,1,0:T(8,128)(2,1)} %copy-done.1, ...), custom_call_target="tpu_custom_call" | custom-call | flops 1000 | bytes 262144 | tf_op jit(solution)/shard_map/dense_backward/pallas_call | solution.py:61
  336.0 5.1 weight_grads.9
  341.1 9.0 %weight_grads.10 = (bf16[2,4,256,512]{3,2,1,0:T(8,128)(2,1)}, bf16[2,4,256,512]{3,2,1,0:T(8,128)(2,1)S(1)}, f32[8,128]{1,0:T(8,128)S(1)}) custom-call(s32[4]{0:T(128)S(1)} %iota_xor_fusion.refs_0_, bf16[592,1024]{1,0:T(8,128)(2,1)S(1)} %get-tuple-element.260.refs_6_.refs_1_, bf16[592,1024]{1,0:T(8,128)(2,1)S(1)} %collective-permute-done.33.refs_2_, ...), custom_call_target="tpu_custom_call" | custom-call | flops 1000 | bytes 262144 | tf_op jit(solution)/shard_map/weight_grads/pallas_call | solution.py:61
  353.4 33.5 %attention_backward.2 = (bf16[5,592,384]{2,1,0:T(8,128)(2,1)}, bf16[5,592,384]{2,1,0:T(8,128)(2,1)}, f32[8,1,384]{2,1,0:T(1,128)S(1)}, bf16[592,1024]{1,0:T(8,12...) custom-call(bf16[2,4,256,512]{3,2,1,0:T(8,128)(2,1)} %copy-done.7, ...), custom_call_target="tpu_custom_call" | custom-call | flops 1000 | bytes 262144 | tf_op jit(solution)/shard_map/attention_backward/pallas_call | solution.py:61
  395.4 10.5 %weight_grads.11 = (bf16[2,4,256,512]{3,2,1,0:T(8,128)(2,1)}, bf16[2,4,256,512]{3,2,1,0:T(8,128)(2,1)S(1)}, f32[8,128]{1,0:T(8,128)S(1)}) custom-call(s32[4]{0:T(128)S(1)} %iota_xor_fusion.refs_0_, bf16[592,1024]{1,0:T(8,128)(2,1)S(1)} %get-tuple-element.281.refs_1_.refs_6_, bf16[592,1024]{1,0:T(8,128)(2,1)} %collective-permute-done.40.refs_2_, ...), custom_call_target="tpu_custom_call" | custom-call | flops 1000 | bytes 262144 | tf_op jit(solution)/shard_map/weight_grads/pallas_call | solution.py:61
  411.0 10.2 %weight_grads.12 = (bf16[2,4,256,384]{3,2,1,0:T(8,128)(2,1)}, bf16[2,4,256,384]{3,2,1,0:T(8,128)(2,1)S(1)}, f32[8,128]{1,0:T(8,128)S(1)}) custom-call(s32[4]{0:T(128)S(1)} %iota_xor_fusion.refs_0_, bf16[592,1024]{1,0:T(8,128)(2,1)} %get-tuple-element.282.refs_1_, bf16[592,1024]{1,0:T(8,128)(2,1)} %collective-permute-done.38.refs_2_, ...), custom_call_target="tpu_custom_call" | custom-call | flops 1000 | bytes 262144 | tf_op jit(solution)/shard_map/weight_grads/pallas_call | solution.py:61
  422.6 21.2 %dense_backward.3 = (bf16[5,592,512]{2,1,0:T(8,128)(2,1)}, bf16[5,592,512]{2,1,0:T(8,128)(2,1)}, f32[8,1,512]{2,1,0:T(1,128)S(1)}, f32[592,1024]{1,0:T(8,128)S(1...) custom-call(bf16[2,4,256,1024]{3,2,1,0:T(8,128)(2,1)} %copy-done, ...), custom_call_target="tpu_custom_call" | custom-call | flops 1000 | bytes 262144 | tf_op jit(solution)/shard_map/dense_backward/pallas_call | solution.py:61
  454.9 5.4 weight_grads.13
  460.3 12.2 %collective-permute-done.44.refs_1_ = bf16[2,4,256,384]{3,2,1,0:T(8,128)(2,1)} collective-permute-done((bf16[2,4,256,384]{3,2,1,0:T(8,128)(2,1)}, bf16[2,4,256,384]{3,2,1,0:T(8,128)(2,1)}, u32[]{:S(2)}, u32[]{:S(2)}) %collective-permute-start.44) | collective-permute-done | bytes 1572896 | tf_op jit(solution)/shard_map/ppermute | solution.py:125
  477.1 10.5 %weight_grads.14 = (bf16[2,4,256,512]{3,2,1,0:T(8,128)(2,1)S(1)}, bf16[2,4,256,512]{3,2,1,0:T(8,128)(2,1)S(1)}, f32[8,128]{1,0:T(8,128)S(1)}) custom-call(s32[4]{0:T(128)S(1)} %iota_xor_fusion.refs_0_, bf16[592,1024]{1,0:T(8,128)(2,1)} %get-tuple-element.231.refs_6_.refs_1_, bf16[592,1024]{1,0:T(8,128)(2,1)} %collective-permute-done.17.refs_2_, ...), custom_call_target="tpu_custom_call" | custom-call | flops 1000 | bytes 262144 | tf_op jit(solution)/shard_map/weight_grads/pallas_call | solution.py:61
  487.9 6.2 collective-permute-done.49.refs_2_
  498.4 33.8 %attention_backward.3 = (bf16[5,592,384]{2,1,0:T(8,128)(2,1)}, bf16[5,592,384]{2,1,0:T(8,128)(2,1)}, f32[8,1,384]{2,1,0:T(1,128)S(1)}, bf16[592,1024]{1,0:T(8,12...) custom-call(bf16[2,4,256,512]{3,2,1,0:T(8,128)(2,1)} %copy-done.6, ...), custom_call_target="tpu_custom_call" | custom-call | flops 1000 | bytes 262144 | tf_op jit(solution)/shard_map/attention_backward/pallas_call | solution.py:61
  536.8 4.4 all-to-all-start
  548.1 9.6 %weight_grads.15 = (bf16[2,4,256,384]{3,2,1,0:T(8,128)(2,1)S(1)}, bf16[2,4,256,384]{3,2,1,0:T(8,128)(2,1)S(1)}, f32[8,128]{1,0:T(8,128)S(1)}) custom-call(s32[4]{0:T(128)S(1)} %iota_xor_fusion.refs_0_, bf16[592,1024]{1,0:T(8,128)(2,1)} %get-tuple-element.230.refs_1_, bf16[592,1024]{1,0:T(8,128)(2,1)} %collective-permute-done.16.refs_2_, ...), custom_call_target="tpu_custom_call" | custom-call | flops 1000 | bytes 262144 | tf_op jit(solution)/shard_map/weight_grads/pallas_call | solution.py:61
  575.2 6.6 %collective-permute-done.58.refs_1_ = bf16[2,4,256,384]{3,2,1,0:T(8,128)(2,1)S(1)} collective-permute-done((bf16[2,4,256,384]{3,2,1,0:T(8,128)(2,1)}, bf16[2,4,256,384]{3,2,1,0:T(8,128)(2,1)S(1)}, u32[]{:S(2)}, u32[]{:S(2)}) %collective-permute-start.58) | collective-permute-done | bytes 1572896 | tf_op jit(solution)/shard_map/ppermute | solution.py:125
  614.8 12.3 %all-to-all-done.1 = bf16[4,256,384]{2,1,0:T(8,128)(2,1)S(1)} async-done(((bf16[4,256,384]{2,1,0:T(8,128)(2,1)}), bf16[4,256,384]{2,1,0:T(8,128)(2,1)S(1)}, u32[]{:S(2)}, u32[]{:S(2)}) %all-to-all-start.1) | async-done | bytes 786464 | tf_op jit(solution)/shard_map/all_to_all | solution.py:1102
  (517 shorter events, 215.2 us)
Async XLA Ops:
  7.2 49.4 %all-gather.9.cloned.1.call-start = ((), (), s32[]{:S(2)}) async-start(), calls=%async_computation.8 | async-start | bytes 1310720 | tf_op jit(solution)/shard_map/all_gather | solution.py:371
  26.1 80.2 %all-gather.11.cloned.1.call-start = ((), (), s32[]{:S(2)}) async-start(), calls=%async_computation.9 | async-start | bytes 2621440 | tf_op jit(solution)/shard_map/all_gather | solution.py:371
  60.2 92.9 %all-gather.13.cloned.1.call-start = ((), (), s32[]{:S(2)}) async-start(), calls=%async_computation.10 | async-start | bytes 1310720 | tf_op jit(solution)/shard_map/all_gather | solution.py:371
  74.9 37.1 %collective-permute-start.6 = (bf16[2,3,256,512]{3,2,1,0:T(8,128)(2,1)}, bf16[2,3,256,512]{3,2,1,0:T(8,128)(2,1)}, u32[]{:S(2)}, u32[]{:S(2)}) collective-permute-start(bf16[2,3,256,512]{3,2,1,0:T(8,128)(2,1)} %get-tuple-element.213.refs_1_), channel_id=1, source_target_pairs={{0,2},{1,3},{2,0},{3,1},{4,6},{5,7},{6,4},{7,5},{8,10},{9,11},{10,... | collective-permute-start | bytes 4718600 | tf_op jit(solution)/shard_map/ppermute | solution.py:125
  76.6 36.9 %collective-permute-start.12 = (bf16[2,1536]{1,0:T(2,128)(2,1)S(1)}, bf16[2,1536]{1,0:T(2,128)(2,1)S(1)}, u32[]{:S(2)}, u32[]{:S(2)}) collective-permute-start(bf16[2,1536]{1,0:T(2,128)(2,1)S(1)} %pad_maximum_fusion.6), channel_id=1, source_target_pairs={{0,12},{4,8},{8,4},{12,0},{1,13},{5,9},{9,5},{13,1},{2,14},{6,10},... | collective-permute-start | bytes 18440 | tf_op jit(solution)/shard_map/ppermute | solution.py:111
  78.6 35.1 %collective-permute-start.11 = (bf16[2,1536]{1,0:T(2,128)(2,1)S(1)}, bf16[2,1536]{1,0:T(2,128)(2,1)S(1)}, u32[]{:S(2)}, u32[]{:S(2)}) collective-permute-start(bf16[2,1536]{1,0:T(2,128)(2,1)S(1)} %pad_maximum_fusion.6), channel_id=1, source_target_pairs={{0,8},{4,12},{8,0},{12,4},{1,9},{5,13},{9,1},{13,5},{2,10},{6,14},... | collective-permute-start | bytes 18440 | tf_op jit(solution)/shard_map/ppermute | solution.py:111
  80.3 38.3 %collective-permute-start.7 = (bf16[2,3,256,512]{3,2,1,0:T(8,128)(2,1)}, bf16[2,3,256,512]{3,2,1,0:T(8,128)(2,1)}, u32[]{:S(2)}, u32[]{:S(2)}) collective-permute-start(bf16[2,3,256,512]{3,2,1,0:T(8,128)(2,1)} %get-tuple-element.213.refs_1_), channel_id=1, source_target_pairs={{0,16},{16,0},{1,17},{17,1},{2,18},{18,2},{3,19},{19,3},{4,20},{20... | collective-permute-start | bytes 4718600 | tf_op jit(solution)/shard_map/ppermute | solution.py:108
  81.2 101.5 %all-gather.15.cloned.1.call-start = ((), (), s32[]{:S(2)}) async-start(), calls=%async_computation.11 | async-start | bytes 2621440 | tf_op jit(solution)/shard_map/all_gather | solution.py:371
  118.1 327.2 %reduce-scatter.4.cloned.1.call-start = ((), (), s32[]{:S(2)}) async-start(), calls=%async_computation.5 | async-start | bytes 1310720 | tf_op jit(solution)/shard_map/reduce_scatter | solution.py:1104
  145.9 50.0 %collective-permute-start.19 = (bf16[2,3,256,1024]{3,2,1,0:T(8,128)(2,1)S(1)}, bf16[2,3,256,1024]{3,2,1,0:T(8,128)(2,1)}, u32[]{:S(2)}, u32[]{:S(2)}) collective-permute-start(bf16[2,3,256,1024]{3,2,1,0:T(8,128)(2,1)S(1)} %get-tuple-element.233.refs_1_), channel_id=1, source_target_pairs={{0,2},{1,3},{2,0},{3,1},{4,6},{5,7},{6,4},{7,5},{8,10},{9,11},{10,... | collective-permute-start | bytes 9437192 | tf_op jit(solution)/shard_map/ppermute | solution.py:125
  156.4 39.5 %collective-permute-start.22 = (bf16[1,3,256,512]{3,2,1,0:T(8,128)(2,1)}, bf16[1,3,256,512]{3,2,1,0:T(8,128)(2,1)}, u32[]{:S(2)}, u32[]{:S(2)}) collective-permute-start(bf16[1,3,256,512]{3,2,1,0:T(8,128)(2,1)} %get-tuple-element.239.refs_0_), channel_id=1, source_target_pairs={{0,1},{1,0},{2,3},{3,2},{4,5},{5,4},{6,7},{7,6},{8,9},{9,8},{10,11... | collective-permute-start | bytes 2359304 | tf_op jit(solution)/shard_map/ppermute | solution.py:125
  159.4 40.9 %collective-permute-start.20 = (bf16[2,3,256,1024]{3,2,1,0:T(8,128)(2,1)S(1)}, bf16[2,3,256,1024]{3,2,1,0:T(8,128)(2,1)}, u32[]{:S(2)}, u32[]{:S(2)}) collective-permute-start(bf16[2,3,256,1024]{3,2,1,0:T(8,128)(2,1)S(1)} %get-tuple-element.233.refs_1_), channel_id=1, source_target_pairs={{0,16},{16,0},{1,17},{17,1},{2,18},{18,2},{3,19},{19,3},{4,20},{20... | collective-permute-start | bytes 9437192 | tf_op jit(solution)/shard_map/ppermute | solution.py:108
  185.0 42.4 %collective-permute-start.26 = (bf16[1,3,256,1024]{3,2,1,0:T(8,128)(2,1)S(1)}, bf16[1,3,256,1024]{3,2,1,0:T(8,128)(2,1)S(1)}, u32[]{:S(2)}, u32[]{:S(2)}) collective-permute-start(bf16[1,3,256,1024]{3,2,1,0:T(8,128)(2,1)S(1)} %get-tuple-element.249.refs_0_), channel_id=1, source_target_pairs={{0,1},{1,0},{2,3},{3,2},{4,5},{5,4},{6,7},{7,6},{8,9},{9,8},{10,11... | collective-permute-start | bytes 4718600 | tf_op jit(solution)/shard_map/ppermute | solution.py:125
  227.7 37.3 %collective-permute-start.27 = (bf16[2,3,256,1024]{3,2,1,0:T(8,128)(2,1)S(1)}, bf16[2,3,256,1024]{3,2,1,0:T(8,128)(2,1)S(1)}, u32[]{:S(2)}, u32[]{:S(2)}) collective-permute-start(bf16[2,3,256,1024]{3,2,1,0:T(8,128)(2,1)S(1)} %get-tuple-element.257.refs_1_), channel_id=1, source_target_pairs={{0,2},{1,3},{2,0},{3,1},{4,6},{5,7},{6,4},{7,5},{8,10},{9,11},{10,... | collective-permute-start | bytes 9437192 | tf_op jit(solution)/shard_map/ppermute | solution.py:125
  228.2 38.5 %collective-permute-start.28 = (bf16[2,3,256,1024]{3,2,1,0:T(8,128)(2,1)S(1)}, bf16[2,3,256,1024]{3,2,1,0:T(8,128)(2,1)}, u32[]{:S(2)}, u32[]{:S(2)}) collective-permute-start(bf16[2,3,256,1024]{3,2,1,0:T(8,128)(2,1)S(1)} %get-tuple-element.257.refs_1_), channel_id=1, source_target_pairs={{0,16},{16,0},{1,17},{17,1},{2,18},{18,2},{3,19},{19,3},{4,20},{20... | collective-permute-start | bytes 9437192 | tf_op jit(solution)/shard_map/ppermute | solution.py:108
  228.7 31.4 %collective-permute-start.30 = (bf16[5,592,512]{2,1,0:T(8,128)(2,1)}, bf16[5,592,512]{2,1,0:T(8,128)(2,1)S(1)}, u32[]{:S(2)}, u32[]{:S(2)}) collective-permute-start(bf16[5,592,512]{2,1,0:T(8,128)(2,1)} %get-tuple-element.263), channel_id=1, source_target_pairs={{0,16},{16,0},{1,17},{17,1},{2,18},{18,2},{3,19},{19,3},{4,20},{20... | collective-permute-start | bytes 9093128 | tf_op jit(solution)/shard_map/ppermute | solution.py:108
  334.2 52.9 %collective-permute-start.43 = (bf16[1,4,256,512]{3,2,1,0:T(8,128)(2,1)}, bf16[1,4,256,512]{3,2,1,0:T(8,128)(2,1)S(1)}, u32[]{:S(2)}, u32[]{:S(2)}) collective-permute-start(bf16[1,4,256,512]{3,2,1,0:T(8,128)(2,1)} %get-tuple-element.290), channel_id=1, source_target_pairs={{0,1},{1,0},{2,3},{3,2},{4,5},{5,4},{6,7},{7,6},{8,9},{9,8},{10,11... | collective-permute-start | bytes 3145736 | tf_op jit(solution)/shard_map/ppermute | solution.py:125
  351.4 40.5 %collective-permute-start.41 = (bf16[2,4,256,512]{3,2,1,0:T(8,128)(2,1)}, bf16[2,4,256,512]{3,2,1,0:T(8,128)(2,1)}, u32[]{:S(2)}, u32[]{:S(2)}) collective-permute-start(bf16[2,4,256,512]{3,2,1,0:T(8,128)(2,1)} %get-tuple-element.287), channel_id=1, source_target_pairs={{0,2},{1,3},{2,0},{3,1},{4,6},{5,7},{6,4},{7,5},{8,10},{9,11},{10,... | collective-permute-start | bytes 6291464 | tf_op jit(solution)/shard_map/ppermute | solution.py:125
  353.0 58.0 %collective-permute-start.38 = (bf16[592,1024]{1,0:T(8,128)(2,1)}, bf16[592,1024]{1,0:T(8,128)(2,1)}, u32[]{:S(2)}, u32[]{:S(2)}) collective-permute-start(bf16[592,1024]{1,0:T(8,128)(2,1)} %get-tuple-element.282.refs_1_), channel_id=1, source_target_pairs={{0,16},{16,0},{1,17},{17,1},{2,18},{18,2},{3,19},{19,3},{4,20},{20... | collective-permute-start | bytes 3637256 | tf_op jit(solution)/shard_map/ppermute | solution.py:108
  353.0 36.0 %collective-permute-start.42 = (bf16[2,4,256,128]{3,2,1,0:T(8,128)(2,1)}, bf16[2,4,256,128]{3,2,1,0:T(8,128)(2,1)}, u32[]{:S(2)}, u32[]{:S(2)}) collective-permute-start(bf16[2,4,256,128]{3,2,1,0:T(8,128)(2,1)} %get-tuple-element.289), channel_id=1, source_target_pairs={{0,2},{1,3},{2,0},{3,1},{4,6},{5,7},{6,4},{7,5},{8,10},{9,11},{10,... | collective-permute-start | bytes 1572872 | tf_op jit(solution)/shard_map/ppermute | solution.py:125
  388.9 169.9 %reduce-scatter.6.cloned.1.call-start = ((), (), s32[]{:S(2)}) async-start(), calls=%async_computation.6 | async-start | bytes 1638400 | tf_op jit(solution)/shard_map/reduce_scatter | solution.py:1104
  407.2 42.5 %collective-permute-start.46 = (bf16[2,4,256,512]{3,2,1,0:T(8,128)(2,1)}, bf16[2,4,256,512]{3,2,1,0:T(8,128)(2,1)}, u32[]{:S(2)}, u32[]{:S(2)}) collective-permute-start(bf16[2,4,256,512]{3,2,1,0:T(8,128)(2,1)} %get-tuple-element.302), channel_id=1, source_target_pairs={{0,2},{1,3},{2,0},{3,1},{4,6},{5,7},{6,4},{7,5},{8,10},{9,11},{10,... | collective-permute-start | bytes 6291464 | tf_op jit(solution)/shard_map/ppermute | solution.py:125
  408.9 36.9 %collective-permute-start.48 = (bf16[1,4,256,512]{3,2,1,0:T(8,128)(2,1)}, bf16[1,4,256,512]{3,2,1,0:T(8,128)(2,1)}, u32[]{:S(2)}, u32[]{:S(2)}) collective-permute-start(bf16[1,4,256,512]{3,2,1,0:T(8,128)(2,1)} %get-tuple-element.304), channel_id=1, source_target_pairs={{0,1},{1,0},{2,3},{3,2},{4,5},{5,4},{6,7},{7,6},{8,9},{9,8},{10,11... | collective-permute-start | bytes 3145736 | tf_op jit(solution)/shard_map/ppermute | solution.py:125
  409.2 36.1 %collective-permute-start.47 = (bf16[1,4,256,128]{3,2,1,0:T(8,128)(2,1)}, bf16[1,4,256,128]{3,2,1,0:T(8,128)(2,1)}, u32[]{:S(2)}, u32[]{:S(2)}) collective-permute-start(bf16[1,4,256,128]{3,2,1,0:T(8,128)(2,1)} %get-tuple-element.303), channel_id=1, source_target_pairs={{0,1},{1,0},{2,3},{3,2},{4,5},{5,4},{6,7},{7,6},{8,9},{9,8},{10,11... | collective-permute-start | bytes 786440 | tf_op jit(solution)/shard_map/ppermute | solution.py:125
  422.3 50.3 %collective-permute-start.44 = (bf16[2,4,256,384]{3,2,1,0:T(8,128)(2,1)}, bf16[2,4,256,384]{3,2,1,0:T(8,128)(2,1)}, u32[]{:S(2)}, u32[]{:S(2)}) collective-permute-start(bf16[2,4,256,384]{3,2,1,0:T(8,128)(2,1)} %get-tuple-element.300), channel_id=1, source_target_pairs={{0,2},{1,3},{2,0},{3,1},{4,6},{5,7},{6,4},{7,5},{8,10},{9,11},{10,... | collective-permute-start | bytes 4718600 | tf_op jit(solution)/shard_map/ppermute | solution.py:125
  445.3 31.8 %collective-permute-start.51 = (bf16[5,592,512]{2,1,0:T(8,128)(2,1)}, bf16[5,592,512]{2,1,0:T(8,128)(2,1)}, u32[]{:S(2)}, u32[]{:S(2)}) collective-permute-start(bf16[5,592,512]{2,1,0:T(8,128)(2,1)} %get-tuple-element.314), channel_id=1, source_target_pairs={{0,16},{16,0},{1,17},{17,1},{2,18},{18,2},{3,19},{19,3},{4,20},{20... | collective-permute-start | bytes 9093128 | tf_op jit(solution)/shard_map/ppermute | solution.py:108
  453.4 40.7 %collective-permute-start.50 = (bf16[1,4,256,512]{3,2,1,0:T(8,128)(2,1)}, bf16[1,4,256,512]{3,2,1,0:T(8,128)(2,1)}, u32[]{:S(2)}, u32[]{:S(2)}) collective-permute-start(bf16[1,4,256,512]{3,2,1,0:T(8,128)(2,1)} %get-tuple-element.312), channel_id=1, source_target_pairs={{0,1},{1,0},{2,3},{3,2},{4,5},{5,4},{6,7},{7,6},{8,9},{9,8},{10,11... | collective-permute-start | bytes 3145736 | tf_op jit(solution)/shard_map/ppermute | solution.py:125
  475.4 57.5 %collective-permute-start.53 = (bf16[2,4,256,128]{3,2,1,0:T(8,128)(2,1)}, bf16[2,4,256,128]{3,2,1,0:T(8,128)(2,1)}, u32[]{:S(2)}, u32[]{:S(2)}) collective-permute-start(bf16[2,4,256,128]{3,2,1,0:T(8,128)(2,1)} %copy-done.83), channel_id=1, source_target_pairs={{0,2},{1,3},{2,0},{3,1},{4,6},{5,7},{6,4},{7,5},{8,10},{9,11},{10,... | collective-permute-start | bytes 1572872 | tf_op jit(solution)/shard_map/ppermute | solution.py:125
  487.6 46.9 %collective-permute-start.55 = (bf16[2,4,256,512]{3,2,1,0:T(8,128)(2,1)S(1)}, bf16[2,4,256,512]{3,2,1,0:T(8,128)(2,1)S(1)}, u32[]{:S(2)}, u32[]{:S(2)}) collective-permute-start(bf16[2,4,256,512]{3,2,1,0:T(8,128)(2,1)S(1)} %get-tuple-element.349), channel_id=1, source_target_pairs={{0,2},{1,3},{2,0},{3,1},{4,6},{5,7},{6,4},{7,5},{8,10},{9,11},{10,... | collective-permute-start | bytes 6291464 | tf_op jit(solution)/shard_map/ppermute | solution.py:125
  536.2 34.5 %collective-permute-start.60 = (bf16[1,4,256,512]{3,2,1,0:T(8,128)(2,1)}, bf16[1,4,256,512]{3,2,1,0:T(8,128)(2,1)}, u32[]{:S(2)}, u32[]{:S(2)}) collective-permute-start(bf16[1,4,256,512]{3,2,1,0:T(8,128)(2,1)} %get-tuple-element.366), channel_id=1, source_target_pairs={{0,1},{1,0},{2,3},{3,2},{4,5},{5,4},{6,7},{7,6},{8,9},{9,8},{10,11... | collective-permute-start | bytes 3145736 | tf_op jit(solution)/shard_map/ppermute | solution.py:125
  536.8 47.3 %all-to-all-start = ((bf16[4,256,896]{2,1,0:T(8,128)(2,1)}), bf16[4,256,896]{2,1,0:T(8,128)(2,1)}, u32[]{:S(2)}, u32[]{:S(2)}) async-start(bf16[4,256,896]{2,1,0:T(8,128)(2,1)} %bitcast.140), calls=%async_computation.2 | async-start | bytes 3670016 | tf_op jit(solution)/shard_map/all_to_all | solution.py:1102
  541.2 73.6 %reduce-scatter.8.cloned.1.call-start = ((), (), s32[]{:S(2)}) async-start(), calls=%async_computation.7 | async-start | bytes 1638400 | tf_op jit(solution)/shard_map/reduce_scatter | solution.py:1104
  (157 other events, 1623.9 us)
Sparse Core Ops, SparseCore 0:
  26.3 30.2 all-gather.8
  60.3 45.9 all-gather.10
  108.5 26.6 all-gather.12
  137.2 45.4 all-gather.14
  389.0 24.5 reduce-scatter.3
  475.5 28.7 reduce-scatter.5
  575.3 34.1 reduce-scatter.7

commit v2 on v1

--- a/solution.py
+++ b/solution.py
@@ -378,6 +378,10 @@
             near = join(lay, *self.state[n])
         self.state[n] = (near, lay.along_bit(near, self.done[n]))
         self.done[n] += 1
+
+    def settle(self, n):
+        near, arrived = self.state[n]
+        self.state[n] = (near, *self.lay.hold(arrived))
 
     def finish(self, n, own):
         lay = self.lay
@@ -1053,9 +1057,11 @@
             gather.step(2)
             lay.absorb(*exchanged)
             own_dense = arrange_dense(lay, raws[2:], raws_other[2:], scalars)
+            gather.settle(2)
             gather.step(3)
             w_dense = gather.finish(1, own_dense[0])
             gather.step(2)
+            gather.step(3)
             pause(lay)
         else:
             w_dense = gather.finish(3, own_dense[1])
@@ -1073,7 +1079,6 @@
         exchanged.append(lay.across_cores(active_sent))
         if layer == 0:
             w_attention = gather.finish(2, own_attention[1])
-            gather.step(3)
             pause(lay)
         kept.append(
             (entry, normed, mixed, attended, logs, middle, normed_two, active, slope, exchanged)

time: 651 us -> 664 us (1.020)
    ppermute x24, waiting for transfers between devices: 52.7 us -> 69.3 us  [along_bit(): return lax.ppermute(value, ALL_AXES, route)]
    ppermute x38, waiting for transfers between devices: 35.1 us -> 20.6 us  [across_cores(): return lax.ppermute(value, 'section', [(0, 1), (1, 0)])]
    unnamed x236 -> x248, local copies, waits for them, and re-layouts: 64 us -> 70.5 us
  transfers between devices with their start and end apart: 79 -> 79, of which waited for: 24 -> 21; matrix products, arithmetic and copies ran while one was open for 5% -> 5% of each run, Pallas kernels for 45% -> 44%
where the time goes in v2:
time: 664 us; the launch traced here: 655 us
  Pallas kernels  319 us (48%)
  waiting for transfers between devices  156 us (23%)
  local copies, waits for them, and re-layouts  85.5 us (13%)
  starting transfers between devices  58.4 us (9%)
  other arithmetic  19.2 us (3%)
  between operations  16.6 us (3%)
    pallas_call x50, Pallas kernels, launch(): pl.pallas_call(ordered, grid_spec=pltpu.PrefetchScalarGridSpec(num_scalar...  319 us
    unnamed x248, local copies, waits for them, and re-layouts  70.5 us
    ppermute x24, waiting for transfers between devices, along_bit(): return lax.ppermute(value, ALL_AXES, route)  69.3 us
    all_gather x4, waiting for transfers between devices, start(): self.state[n] = lax.all_gather(piece, 'shard')  51.4 us
    ppermute x24, starting transfers between devices, along_bit(): return lax.ppermute(value, ALL_AXES, route)  28.8 us
    ppermute x38, waiting for transfers between devices, across_cores(): return lax.ppermute(value, 'section', [(0, 1), (1, 0)])  20.6 us
    all_to_all x2, waiting for transfers between devices, collect(): latest[names] = lax.all_to_all(total, 'shard', 0, 0, tiled=True)  14.5 us
  transfers between devices with their start and end apart: 79, of which 21 were waited for; matrix products, arithmetic and copies ran while one was open for 5% of the time, Pallas kernels for 44%

profile of v2, /device:TPU:0, one launch (start us, length us, event | category | flops | bytes accessed | tf_op | source)
XLA Modules:
  0.0 654.9 jit_solution(17490227764226035486)
XLA Ops:
  21.0 4.3 collective-permute-done.3
  36.7 6.5 arrange_attention.1
  44.6 12.0 %all-gather.9.cloned.1.call-done = bf16[1024,512]{1,0:T(8,128)(2,1)} async-done(((bf16[256,512]{1,0:T(8,128)(2,1)}), bf16[1024,512]{1,0:T(8,128)(2,1)}) %all-gather.9.cloned.1.call-update) | async-done | bytes 1048592 | tf_op jit(solution)/shard_map/all_gather | solution.py:371
  62.6 9.9 %collective-permute-done.4.refs_1_ = bf16[1,3,256,512]{3,2,1,0:T(8,128)(2,1)S(1)} collective-permute-done((bf16[1,3,256,512]{3,2,1,0:T(8,128)(2,1)}, bf16[1,3,256,512]{3,2,1,0:T(8,128)(2,1)S(1)}, u32[]{:S(2)}, u32[]{:S(2)}) %collective-permute-start.4) | collective-permute-done | bytes 786464 | tf_op jit(solution)/shard_map/ppermute | solution.py:125
  82.7 23.7 %all-gather.11.cloned.1.call-done = bf16[1024,1024]{1,0:T(8,128)(2,1)} async-done(((bf16[256,1024]{1,0:T(8,128)(2,1)}), bf16[1024,1024]{1,0:T(8,128)(2,1)}) %all-gather.11.cloned.1.call-update) | async-done | bytes 2097168 | tf_op jit(solution)/shard_map/all_gather | solution.py:371
  114.7 24.9 %attention_forward.2 = (bf16[592,1024]{1,0:T(8,128)(2,1)}, bf16[8,592,384]{2,1,0:T(8,128)(2,1)}, bf16[8,592,128]{2,1,0:T(8,128)(2,1)S(1)}, f32[8,8,592]{2,1,0:T(...) custom-call(bf16[2,4,256,512]{3,2,1,0:T(8,128)(2,1)S(1)} %get-tuple-element.206.refs_0_, ...), custom_call_target="tpu_custom_call" | custom-call | flops 1000 | bytes 262144 | tf_op jit(solution)/shard_map/attention_forward/pallas_call | solution.py:61
  149.0 7.1 %arrange_dense.1 = (bf16[2,4,256,1024]{3,2,1,0:T(8,128)(2,1)S(1)}, bf16[2,4,256,1024]{3,2,1,0:T(8,128)(2,1)S(1)}, f32[8,128]{1,0:T(8,128)S(1)}) custom-call(s32[7]{0:T(128)S(1)} %pad_add_fusion.refs_0_, bf16[1024,1024]{1,0:T(8,128)(2,1)} %bitcast.6.refs_3_.refs_1_, bf16[1024,1024]{1,0:T(8,128)(2,1)} %collective-permute-done.13.refs_2_, ...), custom_call_target="tpu_custom_call" | custom-call | flops 1000 | bytes 262144 | tf_op jit(solution)/shard_map/arrange_dense/pallas_call | solution.py:61
  160.1 5.9 collective-permute-done.20.refs_1_
  166.9 15.7 %all-gather.15.cloned.1.call-done = bf16[1024,1024]{1,0:T(8,128)(2,1)} async-done(((bf16[256,1024]{1,0:T(8,128)(2,1)}), bf16[1024,1024]{1,0:T(8,128)(2,1)}) %all-gather.15.cloned.1.call-update) | async-done | bytes 2097168 | tf_op jit(solution)/shard_map/all_gather | solution.py:371
  193.3 26.5 %collective-permute-done.23.refs_1_ = bf16[1,3,256,1024]{3,2,1,0:T(8,128)(2,1)} collective-permute-done((bf16[1,3,256,1024]{3,2,1,0:T(8,128)(2,1)}, bf16[1,3,256,1024]{3,2,1,0:T(8,128)(2,1)}, u32[]{:S(2)}, u32[]{:S(2)}) %collective-permute-start.23) | collective-permute-done | bytes 1572896 | tf_op jit(solution)/shard_map/ppermute | solution.py:125
  226.6 18.5 %dense_forward.2 = (bf16[5,592,512]{2,1,0:T(8,128)(2,1)S(1)}, bf16[5,592,512]{2,1,0:T(8,128)(2,1)}, bf16[8,592,512]{2,1,0:T(8,128)(2,1)}, bf16[592,1024]{1,0:T(8,128)(2,1)S(1)}, f32[8,128]{1,0:T(8,128)S(1)}) custom-call(bf16[2,4,256,1024]{3,2,1,0:T(8,128)(2,1)} %copy-done, bf16[2,3,256,1024]{3,2,1,0:T(8,128)(2,1)} %copy-done.2, ...), custom_call_target="tpu_custom_call" | custom-call | flops 1000 | bytes 262144 | tf_op jit(solution)/shard_map/dense_forward/pallas_call | solution.py:61
  250.3 24.2 %attention_forward.3 = (bf16[592,1024]{1,0:T(8,128)(2,1)}, bf16[8,592,384]{2,1,0:T(8,128)(2,1)}, bf16[8,592,128]{2,1,0:T(8,128)(2,1)S(1)}, f32[8,8,592]{2,1,0:T(...) custom-call(bf16[2,4,256,512]{3,2,1,0:T(8,128)(2,1)S(1)} %copy-done.8, ...), custom_call_target="tpu_custom_call" | custom-call | flops 1000 | bytes 262144 | tf_op jit(solution)/shard_map/attention_forward/pallas_call | solution.py:61
  282.2 17.3 %dense_forward.3 = (bf16[5,592,512]{2,1,0:T(8,128)(2,1)S(1)}, bf16[5,592,512]{2,1,0:T(8,128)(2,1)}, bf16[8,592,512]{2,1,0:T(8,128)(2,1)}, bf16[592,1024]{1,0:T(8,128)(2,1)S(1)}, f32[8,128]{1,0:T(8,128)S(1)}) custom-call(bf16[2,4,256,1024]{3,2,1,0:T(8,128)(2,1)} %copy-done.1, bf16[2,3,256,1024]{3,2,1,0:T(8,128)(2,1)} %copy-done.3, ...), custom_call_target="tpu_custom_call" | custom-call | flops 1000 | bytes 262144 | tf_op jit(solution)/shard_map/dense_forward/pallas_call | solution.py:61
  300.1 6.5 collective-permute-done.31.refs_2_
  307.0 9.0 %weight_grads.8 = (bf16[2,4,256,512]{3,2,1,0:T(8,128)(2,1)}, bf16[2,4,256,512]{3,2,1,0:T(8,128)(2,1)S(1)}, f32[8,128]{1,0:T(8,128)S(1)}) custom-call(s32[4]{0:T(128)S(1)} %iota_xor_fusion.refs_0_, bf16[592,1024]{1,0:T(8,128)(2,1)S(1)} %copy-done.15, bf16[592,1024]{1,0:T(8,128)(2,1)S(1)} %collective-permute-done.31.refs_2_, ...), custom_call_target="tpu_custom_call" | custom-call | flops 1000 | bytes 262144 | tf_op jit(solution)/shard_map/weight_grads/pallas_call | solution.py:61
  318.4 21.3 %dense_backward.2 = (bf16[5,592,512]{2,1,0:T(8,128)(2,1)}, bf16[5,592,512]{2,1,0:T(8,128)(2,1)}, f32[8,1,512]{2,1,0:T(1,128)S(1)}, f32[592,1024]{1,0:T(8,128)S(1...) custom-call(bf16[2,4,256,1024]{3,2,1,0:T(8,128)(2,1)} %copy-done.1, ...), custom_call_target="tpu_custom_call" | custom-call | flops 1000 | bytes 262144 | tf_op jit(solution)/shard_map/dense_backward/pallas_call | solution.py:61
  348.6 5.1 weight_grads.9
  353.7 9.0 %weight_grads.10 = (bf16[2,4,256,512]{3,2,1,0:T(8,128)(2,1)}, bf16[2,4,256,512]{3,2,1,0:T(8,128)(2,1)S(1)}, f32[8,128]{1,0:T(8,128)S(1)}) custom-call(s32[4]{0:T(128)S(1)} %iota_xor_fusion.refs_0_, bf16[592,1024]{1,0:T(8,128)(2,1)S(1)} %get-tuple-element.264.refs_6_.refs_1_, bf16[592,1024]{1,0:T(8,128)(2,1)S(1)} %collective-permute-done.33.refs_2_, ...), custom_call_target="tpu_custom_call" | custom-call | flops 1000 | bytes 262144 | tf_op jit(solution)/shard_map/weight_grads/pallas_call | solution.py:61
  366.5 33.4 %attention_backward.2 = (bf16[5,592,384]{2,1,0:T(8,128)(2,1)}, bf16[5,592,384]{2,1,0:T(8,128)(2,1)}, f32[8,1,384]{2,1,0:T(1,128)S(1)}, bf16[592,1024]{1,0:T(8,12...) custom-call(bf16[2,4,256,512]{3,2,1,0:T(8,128)(2,1)} %copy-done.7, ...), custom_call_target="tpu_custom_call" | custom-call | flops 1000 | bytes 262144 | tf_op jit(solution)/shard_map/attention_backward/pallas_call | solution.py:61
  408.4 10.5 %weight_grads.11 = (bf16[2,4,256,512]{3,2,1,0:T(8,128)(2,1)}, bf16[2,4,256,512]{3,2,1,0:T(8,128)(2,1)S(1)}, f32[8,128]{1,0:T(8,128)S(1)}) custom-call(s32[4]{0:T(128)S(1)} %iota_xor_fusion.refs_0_, bf16[592,1024]{1,0:T(8,128)(2,1)S(1)} %get-tuple-element.285.refs_1_.refs_6_, bf16[592,1024]{1,0:T(8,128)(2,1)} %collective-permute-done.40.refs_2_, ...), custom_call_target="tpu_custom_call" | custom-call | flops 1000 | bytes 262144 | tf_op jit(solution)/shard_map/weight_grads/pallas_call | solution.py:61
  423.4 10.2 %weight_grads.12 = (bf16[2,4,256,384]{3,2,1,0:T(8,128)(2,1)}, bf16[2,4,256,384]{3,2,1,0:T(8,128)(2,1)S(1)}, f32[8,128]{1,0:T(8,128)S(1)}) custom-call(s32[4]{0:T(128)S(1)} %iota_xor_fusion.refs_0_, bf16[592,1024]{1,0:T(8,128)(2,1)} %get-tuple-element.286.refs_1_, bf16[592,1024]{1,0:T(8,128)(2,1)} %collective-permute-done.38.refs_2_, ...), custom_call_target="tpu_custom_call" | custom-call | flops 1000 | bytes 262144 | tf_op jit(solution)/shard_map/weight_grads/pallas_call | solution.py:61
  435.8 21.2 %dense_backward.3 = (bf16[5,592,512]{2,1,0:T(8,128)(2,1)}, bf16[5,592,512]{2,1,0:T(8,128)(2,1)}, f32[8,1,512]{2,1,0:T(1,128)S(1)}, f32[592,1024]{1,0:T(8,128)S(1...) custom-call(bf16[2,4,256,1024]{3,2,1,0:T(8,128)(2,1)} %copy-done, ...), custom_call_target="tpu_custom_call" | custom-call | flops 1000 | bytes 262144 | tf_op jit(solution)/shard_map/dense_backward/pallas_call | solution.py:61
  467.8 5.4 weight_grads.13
  473.2 12.4 %collective-permute-done.44.refs_1_ = bf16[2,4,256,384]{3,2,1,0:T(8,128)(2,1)} collective-permute-done((bf16[2,4,256,384]{3,2,1,0:T(8,128)(2,1)}, bf16[2,4,256,384]{3,2,1,0:T(8,128)(2,1)}, u32[]{:S(2)}, u32[]{:S(2)}) %collective-permute-start.44) | collective-permute-done | bytes 1572896 | tf_op jit(solution)/shard_map/ppermute | solution.py:125
  490.2 10.4 %weight_grads.14 = (bf16[2,4,256,512]{3,2,1,0:T(8,128)(2,1)S(1)}, bf16[2,4,256,512]{3,2,1,0:T(8,128)(2,1)S(1)}, f32[8,128]{1,0:T(8,128)S(1)}) custom-call(s32[4]{0:T(128)S(1)} %iota_xor_fusion.refs_0_, bf16[592,1024]{1,0:T(8,128)(2,1)} %get-tuple-element.233.refs_6_.refs_1_, bf16[592,1024]{1,0:T(8,128)(2,1)} %collective-permute-done.17.refs_2_, ...), custom_call_target="tpu_custom_call" | custom-call | flops 1000 | bytes 262144 | tf_op jit(solution)/shard_map/weight_grads/pallas_call | solution.py:61
  501.6 5.9 collective-permute-done.49.refs_2_
  511.7 33.8 %attention_backward.3 = (bf16[5,592,384]{2,1,0:T(8,128)(2,1)}, bf16[5,592,384]{2,1,0:T(8,128)(2,1)}, f32[8,1,384]{2,1,0:T(1,128)S(1)}, bf16[592,1024]{1,0:T(8,12...) custom-call(bf16[2,4,256,512]{3,2,1,0:T(8,128)(2,1)} %copy-done.6, ...), custom_call_target="tpu_custom_call" | custom-call | flops 1000 | bytes 262144 | tf_op jit(solution)/shard_map/attention_backward/pallas_call | solution.py:61
  549.6 4.4 all-to-all-start
  561.5 9.6 %weight_grads.15 = (bf16[2,4,256,384]{3,2,1,0:T(8,128)(2,1)S(1)}, bf16[2,4,256,384]{3,2,1,0:T(8,128)(2,1)S(1)}, f32[8,128]{1,0:T(8,128)S(1)}) custom-call(s32[4]{0:T(128)S(1)} %iota_xor_fusion.refs_0_, bf16[592,1024]{1,0:T(8,128)(2,1)} %get-tuple-element.232.refs_1_, bf16[592,1024]{1,0:T(8,128)(2,1)} %collective-permute-done.16.refs_2_, ...), custom_call_target="tpu_custom_call" | custom-call | flops 1000 | bytes 262144 | tf_op jit(solution)/shard_map/weight_grads/pallas_call | solution.py:61
  587.6 6.7 %collective-permute-done.58.refs_1_ = bf16[2,4,256,384]{3,2,1,0:T(8,128)(2,1)S(1)} collective-permute-done((bf16[2,4,256,384]{3,2,1,0:T(8,128)(2,1)}, bf16[2,4,256,384]{3,2,1,0:T(8,128)(2,1)S(1)}, u32[]{:S(2)}, u32[]{:S(2)}) %collective-permute-start.58) | collective-permute-done | bytes 1572896 | tf_op jit(solution)/shard_map/ppermute | solution.py:125
  615.1 5.0 all-to-all-start.1
  627.5 11.9 %all-to-all-done.1 = bf16[4,256,384]{2,1,0:T(8,128)(2,1)S(1)} async-done(((bf16[4,256,384]{2,1,0:T(8,128)(2,1)}), bf16[4,256,384]{2,1,0:T(8,128)(2,1)S(1)}, u32[]{:S(2)}, u32[]{:S(2)}) %all-to-all-start.1) | async-done | bytes 786464 | tf_op jit(solution)/shard_map/all_to_all | solution.py:1107
  (529 shorter events, 210.2 us)
Async XLA Ops:
  7.2 49.4 %all-gather.9.cloned.1.call-start = ((), (), s32[]{:S(2)}) async-start(), calls=%async_computation.8 | async-start | bytes 1310720 | tf_op jit(solution)/shard_map/all_gather | solution.py:371
  26.1 80.2 %all-gather.11.cloned.1.call-start = ((), (), s32[]{:S(2)}) async-start(), calls=%async_computation.9 | async-start | bytes 2621440 | tf_op jit(solution)/shard_map/all_gather | solution.py:371
  60.2 83.3 %all-gather.13.cloned.1.call-start = ((), (), s32[]{:S(2)}) async-start(), calls=%async_computation.10 | async-start | bytes 1310720 | tf_op jit(solution)/shard_map/all_gather | solution.py:371
  74.9 36.0 %collective-permute-start.6 = (bf16[2,3,256,512]{3,2,1,0:T(8,128)(2,1)}, bf16[2,3,256,512]{3,2,1,0:T(8,128)(2,1)}, u32[]{:S(2)}, u32[]{:S(2)}) collective-permute-start(bf16[2,3,256,512]{3,2,1,0:T(8,128)(2,1)} %get-tuple-element.215.refs_1_), channel_id=1, source_target_pairs={{0,2},{1,3},{2,0},{3,1},{4,6},{5,7},{6,4},{7,5},{8,10},{9,11},{10,... | collective-permute-start | bytes 4718600 | tf_op jit(solution)/shard_map/ppermute | solution.py:125
  77.3 105.4 %all-gather.15.cloned.1.call-start = ((), (), s32[]{:S(2)}) async-start(), calls=%async_computation.11 | async-start | bytes 2621440 | tf_op jit(solution)/shard_map/all_gather | solution.py:371
  77.4 33.7 %collective-permute-start.12 = (bf16[2,1536]{1,0:T(2,128)(2,1)S(1)}, bf16[2,1536]{1,0:T(2,128)(2,1)S(1)}, u32[]{:S(2)}, u32[]{:S(2)}) collective-permute-start(bf16[2,1536]{1,0:T(2,128)(2,1)S(1)} %pad_maximum_fusion.6), channel_id=1, source_target_pairs={{0,12},{4,8},{8,4},{12,0},{1,13},{5,9},{9,5},{13,1},{2,14},{6,10},... | collective-permute-start | bytes 18440 | tf_op jit(solution)/shard_map/ppermute | solution.py:111
  79.4 33.3 %collective-permute-start.11 = (bf16[2,1536]{1,0:T(2,128)(2,1)S(1)}, bf16[2,1536]{1,0:T(2,128)(2,1)S(1)}, u32[]{:S(2)}, u32[]{:S(2)}) collective-permute-start(bf16[2,1536]{1,0:T(2,128)(2,1)S(1)} %pad_maximum_fusion.6), channel_id=1, source_target_pairs={{0,8},{4,12},{8,0},{12,4},{1,9},{5,13},{9,1},{13,5},{2,10},{6,14},... | collective-permute-start | bytes 18440 | tf_op jit(solution)/shard_map/ppermute | solution.py:111
  111.1 347.4 %reduce-scatter.4.cloned.1.call-start = ((), (), s32[]{:S(2)}) async-start(), calls=%async_computation.5 | async-start | bytes 1310720 | tf_op jit(solution)/shard_map/reduce_scatter | solution.py:1109
  112.7 36.4 %collective-permute-start.13 = (bf16[1024,1024]{1,0:T(8,128)(2,1)}, bf16[1024,1024]{1,0:T(8,128)(2,1)}, u32[]{:S(2)}, u32[]{:S(2)}) collective-permute-start(bf16[1024,1024]{1,0:T(8,128)(2,1)} %bitcast.6.refs_3_.refs_1_), channel_id=1, source_target_pairs={{0,16},{16,0},{1,17},{17,1},{2,18},{18,2},{3,19},{19,3},{4,20},{20... | collective-permute-start | bytes 6291464 | tf_op jit(solution)/shard_map/ppermute | solution.py:108
  112.9 36.1 %collective-permute-start.14 = (bf16[1024,1024]{1,0:T(8,128)(2,1)}, bf16[1024,1024]{1,0:T(8,128)(2,1)}, u32[]{:S(2)}, u32[]{:S(2)}) collective-permute-start(bf16[1024,1024]{1,0:T(8,128)(2,1)} %bitcast.7.refs_4_.refs_3_), channel_id=1, source_target_pairs={{0,16},{16,0},{1,17},{17,1},{2,18},{18,2},{3,19},{19,3},{4,20},{20... | collective-permute-start | bytes 6291464 | tf_op jit(solution)/shard_map/ppermute | solution.py:108
  142.0 46.8 %collective-permute-start.19 = (bf16[2,3,256,1024]{3,2,1,0:T(8,128)(2,1)S(1)}, bf16[2,3,256,1024]{3,2,1,0:T(8,128)(2,1)}, u32[]{:S(2)}, u32[]{:S(2)}) collective-permute-start(bf16[2,3,256,1024]{3,2,1,0:T(8,128)(2,1)S(1)} %get-tuple-element.235.refs_1_), channel_id=1, source_target_pairs={{0,2},{1,3},{2,0},{3,1},{4,6},{5,7},{6,4},{7,5},{8,10},{9,11},{10,... | collective-permute-start | bytes 9437192 | tf_op jit(solution)/shard_map/ppermute | solution.py:125
  186.4 33.4 %collective-permute-start.23 = (bf16[1,3,256,1024]{3,2,1,0:T(8,128)(2,1)}, bf16[1,3,256,1024]{3,2,1,0:T(8,128)(2,1)}, u32[]{:S(2)}, u32[]{:S(2)}) collective-permute-start(bf16[1,3,256,1024]{3,2,1,0:T(8,128)(2,1)} %get-tuple-element.243.refs_0_), channel_id=1, source_target_pairs={{0,1},{1,0},{2,3},{3,2},{4,5},{5,4},{6,7},{7,6},{8,9},{9,8},{10,11... | collective-permute-start | bytes 4718600 | tf_op jit(solution)/shard_map/ppermute | solution.py:125
  188.7 35.3 %collective-permute-start.21 = (bf16[2,3,256,1024]{3,2,1,0:T(8,128)(2,1)S(1)}, bf16[2,3,256,1024]{3,2,1,0:T(8,128)(2,1)S(1)}, u32[]{:S(2)}, u32[]{:S(2)}) collective-permute-start(bf16[2,3,256,1024]{3,2,1,0:T(8,128)(2,1)S(1)} %get-tuple-element.235.refs_1_), channel_id=1, source_target_pairs={{0,16},{16,0},{1,17},{17,1},{2,18},{18,2},{3,19},{19,3},{4,20},{20... | collective-permute-start | bytes 9437192 | tf_op jit(solution)/shard_map/ppermute | solution.py:108
  191.2 55.5 %collective-permute-start.24 = (bf16[2,3,256,512]{3,2,1,0:T(8,128)(2,1)S(1)}, bf16[2,3,256,512]{3,2,1,0:T(8,128)(2,1)}, u32[]{:S(2)}, u32[]{:S(2)}) collective-permute-start(bf16[2,3,256,512]{3,2,1,0:T(8,128)(2,1)S(1)} %get-tuple-element.251.refs_1_), channel_id=1, source_target_pairs={{0,2},{1,3},{2,0},{3,1},{4,6},{5,7},{6,4},{7,5},{8,10},{9,11},{10,... | collective-permute-start | bytes 4718600 | tf_op jit(solution)/shard_map/ppermute | solution.py:125
  192.7 55.1 %collective-permute-start.25 = (bf16[2,3,256,512]{3,2,1,0:T(8,128)(2,1)S(1)}, bf16[2,3,256,512]{3,2,1,0:T(8,128)(2,1)}, u32[]{:S(2)}, u32[]{:S(2)}) collective-permute-start(bf16[2,3,256,512]{3,2,1,0:T(8,128)(2,1)S(1)} %get-tuple-element.251.refs_1_), channel_id=1, source_target_pairs={{0,16},{16,0},{1,17},{17,1},{2,18},{18,2},{3,19},{19,3},{4,20},{20... | collective-permute-start | bytes 4718600 | tf_op jit(solution)/shard_map/ppermute | solution.py:108
  222.6 52.0 %collective-permute-start.27 = (bf16[2,3,256,1024]{3,2,1,0:T(8,128)(2,1)S(1)}, bf16[2,3,256,1024]{3,2,1,0:T(8,128)(2,1)}, u32[]{:S(2)}, u32[]{:S(2)}) collective-permute-start(bf16[2,3,256,1024]{3,2,1,0:T(8,128)(2,1)S(1)} %get-tuple-element.261.refs_1_), channel_id=1, source_target_pairs={{0,2},{1,3},{2,0},{3,1},{4,6},{5,7},{6,4},{7,5},{8,10},{9,11},{10,... | collective-permute-start | bytes 9437192 | tf_op jit(solution)/shard_map/ppermute | solution.py:125
  224.0 52.3 %collective-permute-start.28 = (bf16[2,3,256,1024]{3,2,1,0:T(8,128)(2,1)S(1)}, bf16[2,3,256,1024]{3,2,1,0:T(8,128)(2,1)}, u32[]{:S(2)}, u32[]{:S(2)}) collective-permute-start(bf16[2,3,256,1024]{3,2,1,0:T(8,128)(2,1)S(1)} %get-tuple-element.261.refs_1_), channel_id=1, source_target_pairs={{0,16},{16,0},{1,17},{17,1},{2,18},{18,2},{3,19},{19,3},{4,20},{20... | collective-permute-start | bytes 9437192 | tf_op jit(solution)/shard_map/ppermute | solution.py:108
  344.8 55.5 %collective-permute-start.43 = (bf16[1,4,256,512]{3,2,1,0:T(8,128)(2,1)}, bf16[1,4,256,512]{3,2,1,0:T(8,128)(2,1)S(1)}, u32[]{:S(2)}, u32[]{:S(2)}) collective-permute-start(bf16[1,4,256,512]{3,2,1,0:T(8,128)(2,1)} %get-tuple-element.294), channel_id=1, source_target_pairs={{0,1},{1,0},{2,3},{3,2},{4,5},{5,4},{6,7},{7,6},{8,9},{9,8},{10,11... | collective-permute-start | bytes 3145736 | tf_op jit(solution)/shard_map/ppermute | solution.py:125
  364.1 40.7 %collective-permute-start.41 = (bf16[2,4,256,512]{3,2,1,0:T(8,128)(2,1)}, bf16[2,4,256,512]{3,2,1,0:T(8,128)(2,1)}, u32[]{:S(2)}, u32[]{:S(2)}) collective-permute-start(bf16[2,4,256,512]{3,2,1,0:T(8,128)(2,1)} %get-tuple-element.291), channel_id=1, source_target_pairs={{0,2},{1,3},{2,0},{3,1},{4,6},{5,7},{6,4},{7,5},{8,10},{9,11},{10,... | collective-permute-start | bytes 6291464 | tf_op jit(solution)/shard_map/ppermute | solution.py:125
  365.1 58.3 %collective-permute-start.38 = (bf16[592,1024]{1,0:T(8,128)(2,1)}, bf16[592,1024]{1,0:T(8,128)(2,1)}, u32[]{:S(2)}, u32[]{:S(2)}) collective-permute-start(bf16[592,1024]{1,0:T(8,128)(2,1)} %get-tuple-element.286.refs_1_), channel_id=1, source_target_pairs={{0,16},{16,0},{1,17},{17,1},{2,18},{18,2},{3,19},{19,3},{4,20},{20... | collective-permute-start | bytes 3637256 | tf_op jit(solution)/shard_map/ppermute | solution.py:108
  365.5 36.4 %collective-permute-start.42 = (bf16[2,4,256,128]{3,2,1,0:T(8,128)(2,1)}, bf16[2,4,256,128]{3,2,1,0:T(8,128)(2,1)}, u32[]{:S(2)}, u32[]{:S(2)}) collective-permute-start(bf16[2,4,256,128]{3,2,1,0:T(8,128)(2,1)} %get-tuple-element.293), channel_id=1, source_target_pairs={{0,2},{1,3},{2,0},{3,1},{4,6},{5,7},{6,4},{7,5},{8,10},{9,11},{10,... | collective-permute-start | bytes 1572872 | tf_op jit(solution)/shard_map/ppermute | solution.py:125
  401.8 170.5 %reduce-scatter.6.cloned.1.call-start = ((), (), s32[]{:S(2)}) async-start(), calls=%async_computation.6 | async-start | bytes 1638400 | tf_op jit(solution)/shard_map/reduce_scatter | solution.py:1109
  420.3 42.6 %collective-permute-start.46 = (bf16[2,4,256,512]{3,2,1,0:T(8,128)(2,1)}, bf16[2,4,256,512]{3,2,1,0:T(8,128)(2,1)}, u32[]{:S(2)}, u32[]{:S(2)}) collective-permute-start(bf16[2,4,256,512]{3,2,1,0:T(8,128)(2,1)} %get-tuple-element.306), channel_id=1, source_target_pairs={{0,2},{1,3},{2,0},{3,1},{4,6},{5,7},{6,4},{7,5},{8,10},{9,11},{10,... | collective-permute-start | bytes 6291464 | tf_op jit(solution)/shard_map/ppermute | solution.py:125
  421.4 37.6 %collective-permute-start.48 = (bf16[1,4,256,512]{3,2,1,0:T(8,128)(2,1)}, bf16[1,4,256,512]{3,2,1,0:T(8,128)(2,1)}, u32[]{:S(2)}, u32[]{:S(2)}) collective-permute-start(bf16[1,4,256,512]{3,2,1,0:T(8,128)(2,1)} %get-tuple-element.308), channel_id=1, source_target_pairs={{0,1},{1,0},{2,3},{3,2},{4,5},{5,4},{6,7},{7,6},{8,9},{9,8},{10,11... | collective-permute-start | bytes 3145736 | tf_op jit(solution)/shard_map/ppermute | solution.py:125
  422.4 36.0 %collective-permute-start.47 = (bf16[1,4,256,128]{3,2,1,0:T(8,128)(2,1)}, bf16[1,4,256,128]{3,2,1,0:T(8,128)(2,1)}, u32[]{:S(2)}, u32[]{:S(2)}) collective-permute-start(bf16[1,4,256,128]{3,2,1,0:T(8,128)(2,1)} %get-tuple-element.307), channel_id=1, source_target_pairs={{0,1},{1,0},{2,3},{3,2},{4,5},{5,4},{6,7},{7,6},{8,9},{9,8},{10,11... | collective-permute-start | bytes 786440 | tf_op jit(solution)/shard_map/ppermute | solution.py:125
  434.7 50.8 %collective-permute-start.44 = (bf16[2,4,256,384]{3,2,1,0:T(8,128)(2,1)}, bf16[2,4,256,384]{3,2,1,0:T(8,128)(2,1)}, u32[]{:S(2)}, u32[]{:S(2)}) collective-permute-start(bf16[2,4,256,384]{3,2,1,0:T(8,128)(2,1)} %get-tuple-element.304), channel_id=1, source_target_pairs={{0,2},{1,3},{2,0},{3,1},{4,6},{5,7},{6,4},{7,5},{8,10},{9,11},{10,... | collective-permute-start | bytes 4718600 | tf_op jit(solution)/shard_map/ppermute | solution.py:125
  466.6 40.9 %collective-permute-start.50 = (bf16[1,4,256,512]{3,2,1,0:T(8,128)(2,1)}, bf16[1,4,256,512]{3,2,1,0:T(8,128)(2,1)}, u32[]{:S(2)}, u32[]{:S(2)}) collective-permute-start(bf16[1,4,256,512]{3,2,1,0:T(8,128)(2,1)} %get-tuple-element.316), channel_id=1, source_target_pairs={{0,1},{1,0},{2,3},{3,2},{4,5},{5,4},{6,7},{7,6},{8,9},{9,8},{10,11... | collective-permute-start | bytes 3145736 | tf_op jit(solution)/shard_map/ppermute | solution.py:125
  489.1 57.2 %collective-permute-start.53 = (bf16[2,4,256,128]{3,2,1,0:T(8,128)(2,1)}, bf16[2,4,256,128]{3,2,1,0:T(8,128)(2,1)}, u32[]{:S(2)}, u32[]{:S(2)}) collective-permute-start(bf16[2,4,256,128]{3,2,1,0:T(8,128)(2,1)} %copy-done.89), channel_id=1, source_target_pairs={{0,2},{1,3},{2,0},{3,1},{4,6},{5,7},{6,4},{7,5},{8,10},{9,11},{10,... | collective-permute-start | bytes 1572872 | tf_op jit(solution)/shard_map/ppermute | solution.py:125
  500.6 47.3 %collective-permute-start.55 = (bf16[2,4,256,512]{3,2,1,0:T(8,128)(2,1)S(1)}, bf16[2,4,256,512]{3,2,1,0:T(8,128)(2,1)S(1)}, u32[]{:S(2)}, u32[]{:S(2)}) collective-permute-start(bf16[2,4,256,512]{3,2,1,0:T(8,128)(2,1)S(1)} %get-tuple-element.353), channel_id=1, source_target_pairs={{0,2},{1,3},{2,0},{3,1},{4,6},{5,7},{6,4},{7,5},{8,10},{9,11},{10,... | collective-permute-start | bytes 6291464 | tf_op jit(solution)/shard_map/ppermute | solution.py:125
  549.6 33.5 %collective-permute-start.60 = (bf16[1,4,256,512]{3,2,1,0:T(8,128)(2,1)}, bf16[1,4,256,512]{3,2,1,0:T(8,128)(2,1)}, u32[]{:S(2)}, u32[]{:S(2)}) collective-permute-start(bf16[1,4,256,512]{3,2,1,0:T(8,128)(2,1)} %get-tuple-element.370), channel_id=1, source_target_pairs={{0,1},{1,0},{2,3},{3,2},{4,5},{5,4},{6,7},{7,6},{8,9},{9,8},{10,11... | collective-permute-start | bytes 3145736 | tf_op jit(solution)/shard_map/ppermute | solution.py:125
  549.6 48.3 %all-to-all-start = ((bf16[4,256,896]{2,1,0:T(8,128)(2,1)}), bf16[4,256,896]{2,1,0:T(8,128)(2,1)}, u32[]{:S(2)}, u32[]{:S(2)}) async-start(bf16[4,256,896]{2,1,0:T(8,128)(2,1)} %bitcast.140), calls=%async_computation.2 | async-start | bytes 3670016 | tf_op jit(solution)/shard_map/all_to_all | solution.py:1107
  554.0 73.5 %reduce-scatter.8.cloned.1.call-start = ((), (), s32[]{:S(2)}) async-start(), calls=%async_computation.7 | async-start | bytes 1638400 | tf_op jit(solution)/shard_map/reduce_scatter | solution.py:1109
  (163 other events, 1736.1 us)
Sparse Core Ops, SparseCore 0:
  26.3 30.2 all-gather.8
  60.3 45.9 all-gather.10
  108.5 26.6 all-gather.12
  137.2 45.4 all-gather.14
  401.9 25.1 reduce-scatter.3
  489.2 28.7 reduce-scatter.5
  587.8 34.3 reduce-scatter.7
